TPU v7x, 32 devices: a whole 2x2x4 slice. The times are simulated.
32 devices in a mesh: batch: 8 (over z, x), tensor: 4 (over y, core).
Axes of the slice: x: 2, y: 2, z: 4, core: 2. Of those that a mesh axis runs over, the one named last changes fastest.
Arguments:
- tokens: bfloat16 [2048, 4096], P(('batch', 'tensor')), may hold values from -6 to 6
- norm_gain: float32 [4096], replicated, may hold values from 0.1 to 1.9
- w_query: bfloat16 [4096, 4096], P(None, 'tensor'), may hold values from -0.09375 to 0.09375
- w_key: bfloat16 [4096, 1024], P(None, 'tensor'), may hold values from -0.25 to 0.25
- w_value: bfloat16 [4096, 1024], P(None, 'tensor'), may hold values from -0.09375 to 0.09375
- w_out: bfloat16 [4096, 4096], P('tensor'), may hold values from -0.25 to 0.25
- prefix_keys: bfloat16 [4096, 1024], P('batch', 'tensor'), may hold values from -6 to 6
- prefix_values: bfloat16 [4096, 1024], P('batch', 'tensor'), may hold values from -6 to 6
- cache_keys: bfloat16 [36864, 1024], P('batch', 'tensor'), may hold values from -160 to 160
- cache_values: bfloat16 [36864, 1024], P('batch', 'tensor'), may hold values from -6 to 6
- cache_lengths: int32 [32], replicated, may hold values from 128 to 2048, as said below
- prefix_used: int32 [32], P('batch'), may hold values from 1024 to 4096
- parents: int32 [32, 64], P('batch'), may hold values from 0 to 62, as said below
- accepted_index: int32 [32, 8], P('batch'), may hold values from 0 to 63, as said below
Outputs:
- mixed_output: bfloat16 [2048, 4096], P(('batch', 'tensor'))
- accepted_keys: bfloat16 [32, 8, 1024], P('batch', None, 'tensor')
- accepted_values: bfloat16 [32, 8, 1024], P('batch', None, 'tensor')
Inputs may be any that keep to these rules, and one draw needn't show every extreme that they name: `cache_lengths`: within each aligned group of 4 requests at most 2 have more than 256 cached tokens; in the first group exactly that many do, and some request has exactly 2048. parents[r, 0] = 0; for i >= 1, parents[r, i] lies between max(0, i - 8) and i - 1. `accepted_index`: each row lists 8 tree positions, each the parent of the next, ending at a position of 32 or more; where the root is reached the row repeats 0 at its front.
All inputs are finite; a program needn't handle non-finite values.
Results may differ from a plain program's by a relative error of at most 0.015.
The roundings to bfloat16 on the way count: a program that leaves them out, or rounds other values in their place, can miss the bound.
Values may be sent and summed in bfloat16 or wider, within the bound.
No kernel may reach another device: no remote copies, remote signals or barrier semaphores. Data moves between devices by JAX's collectives and lax.ppermute only.
A program may use at most 192 MiB of HBM per device.

v0:
```python
import functools

import jax
import jax.numpy as jnp
from jax import lax
from jax.experimental import pallas as pl
from jax.experimental.pallas import tpu as pltpu
from jax.sharding import PartitionSpec as P

HD = 128
NEG_FILL = -1e30
LOG2E = 1.4426950408889634
AXES = ("batch", "tensor")
SCALE = HD**-0.5 * LOG2E
COST = 1.1e9
HBM = pl.BlockSpec(memory_space=pltpu.HBM)
VMEM = pl.BlockSpec(memory_space=pltpu.VMEM)
SMEM = pl.BlockSpec(memory_space=pltpu.SMEM)


def call(kernel, in_specs, args, out_shape, scratch, megabytes, microseconds, name, after=()):
    n_in, n_out = len(args), len(out_shape)

    def wrapped(*refs):
        kernel(*refs[:n_in], *refs[n_in + len(after) :])

    return pl.pallas_call(
        wrapped,
        in_specs=in_specs + [HBM] * len(after),
        out_specs=[VMEM] * n_out,
        out_shape=out_shape,
        scratch_shapes=scratch,
        compiler_params=pltpu.CompilerParams(vmem_limit_bytes=megabytes * 2**20),
        cost_estimate=pl.CostEstimate(flops=int(microseconds * COST), bytes_accessed=0, transcendentals=0),
        name=name,
    )(*args, *after)


def dot_nt(a, b):
    return lax.dot_general(a, b, (((1,), (1,)), ((), ())), preferred_element_type=jnp.float32)


def head_cols(h):
    return slice(h * HD, (h + 1) * HD)


def fetch_all(sources, held, sems):
    copies = [pltpu.make_async_copy(src, held.at[i], sems.at[i]) for i, src in enumerate(sources)]
    for copy in copies:
        copy.start()
    return copies


def qkv_kernel(n_tok, n_heads, kv_local, steps, *refs):
    token_refs = refs[:n_tok]
    gain_ref, cos_ref, sin_ref = refs[n_tok : n_tok + 3]
    weights = refs[n_tok + 3 : n_tok + 6]
    q_out, k_out, v_out, held, normed, acc, wq, wk, wv, sems, weight_sems = refs[n_tok + 6 :]
    copies = fetch_all(token_refs, held, sems)
    depth = wq.shape[0] // steps
    chunks = []
    for s in range(steps):
        span = slice(s * depth, (s + 1) * depth)
        chunks.append(
            [
                pltpu.make_async_copy(src.at[span], dst.at[span], weight_sems.at[s, i])
                for i, (src, dst) in enumerate(zip(weights, (wq, wk, wv)))
            ]
        )
        for copy in chunks[-1]:
            copy.start()
    rows = held.shape[1]
    step = min(16, rows)
    for i in range(n_tok):
        copies[i].wait()
        for lo in range(0, rows, step):
            values = held[i, lo : lo + step].astype(jnp.float32)
            factor = lax.rsqrt(jnp.mean(values * values, axis=-1, keepdims=True) + 1e-05)
            normed[i * rows + lo : i * rows + lo + step] = (values * factor * gain_ref[...]).astype(jnp.bfloat16)
    cosine = cos_ref[...]
    sine = sin_ref[...]
    reqs, tree = q_out.shape[0], q_out.shape[2]

    def rotated(raw):
        return (raw * cosine + pltpu.roll(raw, HD // 2, 1) * sine).astype(jnp.bfloat16)

    for s in range(steps):
        for copy in chunks[s]:
            copy.wait()
        span = slice(s * depth, (s + 1) * depth)
        x = normed[:, span]
        lo = 0
        for which, w in enumerate((wq, wk, wv)):
            width = w.shape[1]
            raw = jnp.dot(x, w[span], preferred_element_type=jnp.float32)
            if s > 0:
                raw = acc[:, lo : lo + width] + raw
            if s < steps - 1:
                acc[:, lo : lo + width] = raw
            elif which == 0:
                for head in range(n_heads):
                    out = rotated(raw[:, head_cols(head)])
                    for r in range(reqs):
                        q_out[r, head] = out[r * tree : (r + 1) * tree]
            elif which == 1:
                for head in range(kv_local):
                    k_out[:, head_cols(head)] = rotated(raw[:, head_cols(head)])
            else:
                v_out[...] = raw.astype(jnp.bfloat16)
            lo += width


def project(token_list, gain, cosine, sine, w_query, w_key, w_value, tree, after=()):
    rows, width = token_list[0].shape
    n_tok = len(token_list)
    total = rows * n_tok
    n_heads = w_query.shape[1] // HD
    cols = w_key.shape[1]
    steps = 4
    return call(
        functools.partial(qkv_kernel, n_tok, n_heads, cols // HD, steps),
        [HBM] * n_tok + [VMEM] * 3 + [HBM] * 3,
        [*token_list, gain, cosine, sine, w_query, w_key, w_value],
        [
            jax.ShapeDtypeStruct((total // tree, n_heads, tree, HD), jnp.bfloat16),
            jax.ShapeDtypeStruct((total, cols), jnp.bfloat16),
            jax.ShapeDtypeStruct((total, cols), jnp.bfloat16),
        ],
        [
            pltpu.VMEM((n_tok, rows, width), jnp.bfloat16),
            pltpu.VMEM((total, width), jnp.bfloat16),
            pltpu.VMEM((total, w_query.shape[1] + 2 * cols), jnp.float32),
            pltpu.VMEM(w_query.shape, jnp.bfloat16),
            pltpu.VMEM(w_key.shape, jnp.bfloat16),
            pltpu.VMEM(w_value.shape, jnp.bfloat16),
            pltpu.SemaphoreType.DMA((n_tok,)),
            pltpu.SemaphoreType.DMA((steps, 3)),
        ],
        50,
        7,
        "project",
        after,
    )


def absorb(carry, scores, biases, v):
    chunks = []
    for s, bias in zip(scores, biases):
        s = s + bias
        chunks += [s[:, j : j + HD] for j in range(0, s.shape[1], HD)]
    top = chunks[0]
    for c in chunks[1:]:
        top = jnp.maximum(top, c)
    m_new = jnp.broadcast_to(jnp.max(top, axis=1, keepdims=True) * SCALE, top.shape)
    if carry is not None:
        m_new = jnp.maximum(carry[0], m_new)
    total = None
    rounded = []
    for c in chunks:
        w = jnp.exp2(c * SCALE - m_new)
        total = w if total is None else total + w
        rounded.append(w.astype(jnp.bfloat16))
    out = jnp.dot(jnp.concatenate(rounded, axis=1), v, preferred_element_type=jnp.float32)
    if carry is not None:
        alpha = jnp.exp2(carry[0] - m_new)
        total = carry[1] * alpha + total
        out = carry[2] * alpha + out
    return m_new, total, out


def fold_heads(q_ref, slot, kv_local, keys, values, bias, load, store):
    group, tree = q_ref.shape[1] // kv_local, q_ref.shape[2]
    rows = group * tree

    def scores_of(h):
        q = q_ref[slot, h * group : (h + 1) * group].reshape(rows, HD)
        return [dot_nt(q, k(h)) for k in keys]

    def values_of(h):
        parts = [v(h) for v in values]
        return parts[0] if len(parts) == 1 else jnp.concatenate(parts, axis=0)

    ahead = scores_of(0)
    for h in range(kv_local):
        now = ahead
        if h + 1 < kv_local:
            ahead = scores_of(h + 1)
        store(h, absorb(load(h), now, bias, values_of(h)))


def state_access(refs, r):
    def load(h):
        return tuple(ref[r, h] for ref in refs)

    def store(h, state):
        for ref, value in zip(refs, state):
            ref[r, h] = value

    return load, store


def fold_shards(q_ref, r, offset, kv_local, used, bases, base0, held, groups, states):
    n = held.shape[0] // 2
    count = held.shape[1]
    load, store = state_access(states, r)
    for group in groups:
        visible = [used - bases[base0 + i] for i in group]
        most = visible[0]
        for other in visible[1:]:
            most = jnp.maximum(most, other)

        @pl.when(most > 0)
        def _():
            slots = lax.broadcasted_iota(jnp.int32, (1, count), 1)
            fold_heads(
                q_ref,
                offset + r,
                kv_local,
                [lambda h, i=i: held[i, :, head_cols(h)] for i in group],
                [lambda h, i=i: held[n + i, :, head_cols(h)] for i in group],
                [jnp.where(slots < v, 0.0, NEG_FILL) for v in visible],
                load,
                store,
            )


def pairs_of(n):
    return [tuple(range(i, min(i + 2, n))) for i in range(0, n, 2)]


def first_kernel(kv_local, near, block, n_shards, offset, base0, info, bases, q_ref, kn_ref, vn_ref, anc_ref, ck_ref, cv_ref, *refs):
    sources = refs[: 2 * n_shards]
    m_out, l_out, acc_out, k_near, v_near, held, sems = refs[-7:]
    states = (m_out, l_out, acc_out)
    copies = fetch_all(sources, held, sems)
    reqs = m_out.shape[0]
    n_heads, tree = q_ref.shape[1:3]
    group = n_heads // kv_local
    capacity = ck_ref.shape[0]
    for copy in copies:
        copy.wait()
    def one_request(r, _):
        load, store = state_access(states, r)
        low = info[0, offset + r]
        high = info[1, offset + r]
        start0 = pl.multiple_of(jnp.minimum((low // 16) * 16, capacity - near), 16)
        own_rows = pl.ds(pl.multiple_of((offset + r) * tree, tree), tree)
        k_near[0:tree] = kn_ref[own_rows, :]
        v_near[0:tree] = vn_ref[own_rows, :]
        k_near[tree : tree + near] = ck_ref[pl.ds(start0, near), :]
        v_near[tree : tree + near] = cv_ref[pl.ds(start0, near), :]
        column = lax.broadcasted_iota(jnp.int32, (tree, tree + near), 1)
        slots = column - tree + start0
        seen = ((slots >= low) & (slots < high)).astype(jnp.float32)
        linked = jnp.concatenate([anc_ref[offset + r], jnp.zeros((tree, tree + near - HD), jnp.float32)], axis=1)
        bias = jnp.where(jnp.where(column < tree, linked, seen) > 0.5, 0.0, NEG_FILL)
        bias = jnp.concatenate([bias] * group, axis=0)
        seen = [info[2, offset + r] - bases[base0 + i] for i in range(n_shards)]
        place = lax.broadcasted_iota(jnp.int32, (1, held.shape[1]), 1)
        fold_heads(
            q_ref,
            offset + r,
            kv_local,
            [lambda h: k_near[:, head_cols(h)]] + [lambda h, i=i: held[i, :, head_cols(h)] for i in range(n_shards)],
            [lambda h: v_near[:, head_cols(h)]]
            + [lambda h, i=i: held[n_shards + i, :, head_cols(h)] for i in range(n_shards)],
            [bias] + [jnp.where(place < count, 0.0, NEG_FILL) for count in seen],
            lambda h: None,
            store,
        )
        begin0 = start0 + near

        def step(i, _):
            begin = begin0 + i * block
            start = pl.multiple_of(jnp.minimum(begin, capacity - block), 16)
            place = start + lax.broadcasted_iota(jnp.int32, (1, block), 1)
            mask = jnp.where((place >= begin) & (place < high), 0.0, NEG_FILL)
            fold_heads(
                q_ref,
                offset + r,
                kv_local,
                [lambda h: ck_ref[pl.ds(start, block), head_cols(h)]],
                [lambda h: cv_ref[pl.ds(start, block), head_cols(h)]],
                [mask],
                load,
                store,
            )
            return 0

        lax.fori_loop(0, (jnp.maximum(high - begin0, 0) + block - 1) // block, step, 0)
        return 0

    lax.fori_loop(0, reqs, one_request, 0)


def state_shapes(reqs, kv_local, rows):
    return [jax.ShapeDtypeStruct((reqs, kv_local, rows, HD), jnp.float32)] * 3


def shard_scratch(shards):
    n = 2 * len(shards)
    return [pltpu.VMEM((n,) + shards[0][0].shape, jnp.bfloat16), pltpu.SemaphoreType.DMA((n,))]


def flat(shards):
    return [k for k, _ in shards] + [v for _, v in shards]


def attend_first(parts, ancestry, cache_keys, cache_values, info, bases, shards, span, offset, reqs, after=()):
    queries, new_keys, new_values = parts
    shards = shards[span[0] : span[1]]
    _, n_heads, tree, _ = queries.shape
    capacity, cols = cache_keys.shape
    kv_local = cols // HD
    near = min(384 - tree, capacity)
    block = min(1792, capacity)
    n = len(shards)
    return call(
        functools.partial(first_kernel, kv_local, near, block, n, offset, span[0]),
        [SMEM] * 2 + [VMEM] * 6 + [HBM] * (2 * n),
        [info, bases, queries, new_keys, new_values, ancestry, cache_keys, cache_values, *flat(shards)],
        state_shapes(reqs, kv_local, n_heads // kv_local * tree),
        [pltpu.VMEM((tree + near, cols), jnp.bfloat16)] * 2 + shard_scratch(shards),
        40,
        6,
        "attend_first",
        after,
    )


def middle_kernel(kv_local, n_shards, offset, groups, base0, info, bases, q_ref, *refs):
    sources = refs[: 2 * n_shards]
    ins = refs[2 * n_shards : 2 * n_shards + 3]
    outs = refs[2 * n_shards + 3 : 2 * n_shards + 6]
    held, sems = refs[2 * n_shards + 6 :]
    copies = fetch_all(sources, held, sems)
    reqs = outs[0].shape[0]
    for src, dst in zip(ins, outs):
        dst[...] = src[offset : offset + reqs]
    for copy in copies:
        copy.wait()

    def one_request(r, _):
        fold_shards(q_ref, r, offset, kv_local, info[2, offset + r], bases, base0, held, groups, outs)
        return 0

    lax.fori_loop(0, reqs, one_request, 0)


def attend_middle(queries, info, bases, shards, span, state, offset, reqs):
    shards = shards[span[0] : span[1]]
    _, n_heads, tree, _ = queries.shape
    kv_local = shards[0][0].shape[1] // HD
    n = len(shards)
    return call(
        functools.partial(middle_kernel, kv_local, n, offset, pairs_of(n), span[0]),
        [SMEM] * 2 + [VMEM] + [HBM] * (2 * n) + [VMEM] * 3,
        [info, bases, queries, *flat(shards), *state],
        state_shapes(reqs, kv_local, n_heads // kv_local * tree),
        shard_scratch(shards),
        40,
        0.3 + 0.2 * n * reqs,
        "attend_middle",
    )


def last_kernel(kv_local, n_shards, offset, groups, base0, block, info, bases, q_ref, *refs):
    sources = refs[: 2 * n_shards]
    ins = refs[2 * n_shards : 2 * n_shards + 3]
    w_ref = refs[2 * n_shards + 3]
    m_s, l_s, acc_s, attended, w_held, w_sems, held, sems = refs[-8:]
    reqs = m_s.shape[0]
    n_heads, tree = q_ref.shape[1:3]
    outs = refs[-8 - reqs : -8]
    states = (m_s, l_s, acc_s)
    group = n_heads // kv_local
    copies = fetch_all(sources, held, sems)
    cuts = [slice(lo, lo + block) for lo in range(0, w_ref.shape[1], block)]
    w_copies = fetch_all([w_ref.at[:, cut] for cut in cuts], w_held, w_sems)
    for src, dst in zip(ins, states):
        lead = 0 if src.shape[0] == reqs else offset
        dst[...] = src[lead : lead + reqs]
    for copy in copies:
        copy.wait()

    def one_request(r, _):
        fold_shards(q_ref, r, offset, kv_local, info[2, offset + r], bases, base0, held, groups, states)
        for h in range(kv_local):
            total = jnp.sum(l_s[r, h], axis=1, keepdims=True)
            result = (acc_s[r, h] / total).astype(jnp.bfloat16)
            for g in range(group):
                attended[r, :, head_cols(h * group + g)] = result[g * tree : (g + 1) * tree]
        return 0

    lax.fori_loop(0, reqs, one_request, 0)
    x = attended[...].reshape(reqs * tree, n_heads * HD)
    for i, cut in enumerate(cuts):
        w_copies[i].wait()
        product = jnp.dot(x, w_held[i], preferred_element_type=jnp.float32).astype(jnp.bfloat16)
        for r in range(reqs):
            outs[r][:, cut] = product[r * tree : (r + 1) * tree]


def attend_last(queries, info, bases, shards, span, state, w_out, offset, reqs, after=()):
    shards = shards[span[0] : span[1]]
    _, n_heads, tree, _ = queries.shape
    kv_local = shards[0][0].shape[1] // HD
    rows = n_heads // kv_local * tree
    n = len(shards)
    depth, width = w_out.shape
    block = min(1024, width)
    return call(
        functools.partial(last_kernel, kv_local, n, offset, pairs_of(n), span[0], block),
        [SMEM] * 2 + [VMEM] + [HBM] * (2 * n) + [VMEM] * 3 + [HBM],
        [info, bases, queries, *flat(shards), *state, w_out],
        [jax.ShapeDtypeStruct((tree, width), jnp.bfloat16)] * reqs,
        [pltpu.VMEM((reqs, kv_local, rows, HD), jnp.float32)] * 3
        + [
            pltpu.VMEM((reqs, tree, n_heads * HD), jnp.bfloat16),
            pltpu.VMEM((width // block, depth, block), jnp.bfloat16),
            pltpu.SemaphoreType.DMA((width // block,)),
        ]
        + shard_scratch(shards),
        50,
        3.5 + 0.4 * n * reqs,
        "attend_last",
        after,
    )


def add_kernel(*refs):
    total = refs[0][...].astype(jnp.float32)
    for ref in refs[1:-1]:
        total = total + ref[...].astype(jnp.float32)
    refs[-1][...] = total.astype(refs[-1].dtype)


def add_up(*terms, dtype=jnp.bfloat16):
    outs = call(
        add_kernel,
        [VMEM] * len(terms),
        list(terms),
        [jax.ShapeDtypeStruct(terms[0].shape, dtype)],
        [],
        8,
        1,
        "add_up",
    )
    return outs[0]


def ancestor_table(parents):
    node_count = parents.shape[-1]
    column = jnp.arange(node_count, dtype=jnp.int32)
    linked = (parents[..., None] == column) | (column[:, None] == column[None, :])
    ancestry = linked.astype(jnp.bfloat16)
    for repeat in range((node_count - 1).bit_length()):
        paths = jnp.einsum("rij,rjk->rik", ancestry, ancestry, preferred_element_type=jnp.float32)
        ancestry = jnp.minimum(paths, 1.0).astype(jnp.bfloat16)
    return ancestry.astype(jnp.float32)


def rotary_tables(position):
    half = HD // 2
    frequency = 10000.0 ** (-jnp.arange(half, dtype=jnp.float32) / half)
    angles = position.astype(jnp.float32)[:, None] * frequency[None, :]
    cosine = jnp.cos(angles)
    sine = jnp.sin(angles)
    return jnp.concatenate([cosine, cosine], axis=1), jnp.concatenate([-sine, sine], axis=1)


def swap_pairs(batch, tensor, move):
    columns = 2
    pairs = []
    for z in range(batch // columns):
        for x in range(columns):
            for t in range(tensor):
                z2, x2, t2 = move(z, x, t)
                pairs.append(((z * columns + x) * tensor + t, (z2 * columns + x2) * tensor + t2))
    return pairs


def body(
    sizes,
    tokens,
    norm_gain,
    w_query,
    w_key,
    w_value,
    w_out,
    prefix_keys,
    prefix_values,
    cache_keys,
    cache_values,
    cache_lengths,
    prefix_used,
    parents,
    accepted_index,
):
    batch, tensor = sizes
    reqs, tree = parents.shape
    shard_rows = prefix_keys.shape[0]
    fast = sizes == (8, 4) and reqs == tensor and tokens.shape[0] == tree
    me_batch = lax.axis_index("batch")
    me_tensor = lax.axis_index("tensor")
    slots = jnp.arange(reqs, dtype=jnp.int32)

    if fast:
        pairs = functools.partial(swap_pairs, batch, tensor)
        core_pairs = pairs(lambda z, x, t: (z, x, t ^ 1))
        y_pairs = pairs(lambda z, x, t: (z, x, t ^ 2))
        x_pairs = pairs(lambda z, x, t: (z, 1 - x, t))
        z_pairs = pairs(lambda z, x, t: ((z + 1) % (batch // 2), x, t))
        send = lambda a, p: lax.ppermute(a, AXES, p)
        core_tokens = send(tokens, core_pairs)
        y_tokens = send(tokens, y_pairs)
        far_tokens = send(y_tokens, core_pairs)
    order = slots ^ me_tensor if fast else slots
    pick = order[:, None] == slots[None, :]
    own_lengths = lax.dynamic_slice_in_dim(cache_lengths, me_batch * reqs, reqs)
    lower = jnp.cumsum(own_lengths) - own_lengths
    table = jnp.stack([lower, lower + own_lengths, prefix_used])
    info = jnp.sum(jnp.where(pick[None], table[:, None, :], 0), axis=2)
    tree_parents = jnp.sum(jnp.where(pick[:, :, None], parents[None], 0), axis=1)
    ancestry = ancestor_table(tree_parents)
    tree_depth = (jnp.sum(ancestry, axis=-1) - 1.0).astype(jnp.int32)
    position = ((info[2] + info[1] - info[0])[:, None] + tree_depth).reshape(reqs * tree)
    if fast:
        steps = batch // 2
        own_keys, own_values, _ = lax.optimization_barrier((prefix_keys, prefix_values, own_lengths))
        ring = [(prefix_keys, prefix_values)]
        ring.append((send(own_keys, z_pairs), send(own_values, z_pairs)))
        side = [(send(own_keys, x_pairs), send(own_values, x_pairs))]
    cosine, sine = rotary_tables(position)
    ancestry = jnp.pad(ancestry, ((0, 0), (0, 0), (0, HD - tree)))
    shard_ids = jnp.arange(batch, dtype=jnp.int32)
    if fast:
        z, x = me_batch // 2, me_batch % 2
        shard_ids = (z - shard_ids // 2) % (batch // 2) * 2 + (x ^ (shard_ids % 2))
    bases = (shard_ids * shard_rows).astype(jnp.int32)

    def projected(token_list, after=()):
        return project(token_list, norm_gain[None, :], cosine, sine, w_query, w_key, w_value, tree, after)

    if fast:
        def pass_on(step, after):
            keys, values, _ = lax.optimization_barrier((*ring[step], after))
            if step < steps - 1:
                ring.append((send(keys, z_pairs), send(values, z_pairs)))
                side.append((send(keys, x_pairs), send(values, x_pairs)))
            else:
                side.append((send(keys, x_pairs), send(side[-1][1], z_pairs)))

        pass_on(1, cosine)
        parts = projected([tokens, core_tokens, y_tokens, far_tokens])
        queries, new_keys, new_values = parts
        pass_on(2, queries)
        shards = [shard for s in range(steps - 1) for shard in (ring[s], side[s])]
        first = functools.partial(
            attend_first,
            (queries, new_keys, new_values),
            ancestry,
            cache_keys,
            cache_values,
            info,
            bases,
            shards,
            (0, 2),
            reqs=reqs,
        )
        state = first(offset=0)
        pass_on(steps - 1, state[0])
        shards += [ring[-1], side[-1]]
        n = len(shards)
        state = attend_middle(queries, info, bases, shards, (2, 5), state, 0, reqs)
        far_state = attend_middle(queries, info, bases, shards, (5, n - 1), state, 2, 2)
        final = functools.partial(attend_last, queries, info, bases, shards, w_out=w_out, reqs=2)
        kept, away = final((n - 1, n), far_state, offset=2)
        got = send(away, core_pairs)
        summed = add_up(kept, got)
        far = send(summed, y_pairs)
        kept, away = final((5, n), state, offset=0, after=(summed,))
        got = send(away, core_pairs)
        mixed_rows = add_up(add_up(kept, far, dtype=jnp.float32), got)
    else:
        gathered = lax.all_gather(tokens, "tensor", axis=0, tiled=True)
        parts = projected([gathered])
        queries, new_keys, new_values = parts
        all_keys = lax.all_gather(prefix_keys, "batch", axis=0, tiled=True)
        all_values = lax.all_gather(prefix_values, "batch", axis=0, tiled=True)
        split = lambda a: [a[i * shard_rows : (i + 1) * shard_rows] for i in range(batch)]
        shards = list(zip(split(all_keys), split(all_values)))
        state = attend_first(parts, ancestry, cache_keys, cache_values, info, bases, shards, (0, 2), 0, reqs)
        for s in range(2, batch - 2, 4):
            state = attend_middle(queries, info, bases, shards, (s, min(s + 4, batch - 2)), state, 0, reqs)
        partial = attend_last(queries, info, bases, shards, (batch - 2, batch), state, w_out, 0, reqs)
        mixed_rows = lax.psum_scatter(
            jnp.concatenate(partial, axis=0), "tensor", scatter_dimension=0, tiled=True
        )
    rows = ((slots ^ me_tensor if fast else slots)[:, None] * tree + accepted_index).reshape(-1)
    accepted_keys = jnp.take(new_keys, rows, axis=0).reshape(reqs, accepted_index.shape[1], -1)
    accepted_values = jnp.take(new_values, rows, axis=0).reshape(reqs, accepted_index.shape[1], -1)
    return (mixed_rows, accepted_keys, accepted_values)


def solution(mesh):
    sizes = (mesh.shape["batch"], mesh.shape["tensor"])
    in_specs = (
        P(("batch", "tensor"), None),
        P(),
        P(None, "tensor"),
        P(None, "tensor"),
        P(None, "tensor"),
        P("tensor", None),
        P("batch", "tensor"),
        P("batch", "tensor"),
        P("batch", "tensor"),
        P("batch", "tensor"),
        P(),
        P("batch"),
        P("batch", None),
        P("batch", None),
    )
    out_specs = (
        P(("batch", "tensor"), None),
        P("batch", None, "tensor"),
        P("batch", None, "tensor"),
    )
    return jax.shard_map(
        functools.partial(body, sizes), mesh=mesh, in_specs=in_specs, out_specs=out_specs, check_vma=False
    )
```

profile of v0, /device:TPU:0, one launch (start us, length us, event | category | flops | bytes accessed | tf_op | source)
XLA Modules:
  0.0 85.4 jit_solution(7700622819045499530)
XLA Ops:
  0.6 3.0 %collective-permute-start.1 = (bf16[64,4096]{1,0:T(8,128)(2,1)}, bf16[64,4096]{1,0:T(8,128)(2,1)S(1)}, u32[]{:S(2)}, u32[]{:S(2)}) collective-permute-start(bf16[64,4096]{1,0:T(8,128)(2,1)} %refs_0_.1), channel_id=1, source_target_pairs={{0,2},{1,3},{2,0},{3,1},{4,6},{5,7},{6,4},{7,5},{8,10},{9,11},{10,... | collective-permute-start | bytes 1572872 | tf_op jit(solution)/shard_map/ppermute | solution.py:514
  3.7 1.5 %collective-permute-start.10 = (bf16[512,256]{1,0:T(8,128)(2,1)}, bf16[512,256]{1,0:T(8,128)(2,1)S(1)}, u32[]{:S(2)}, u32[]{:S(2)}) collective-permute-start(bf16[512,256]{1,0:T(8,128)(2,1)} %refs_8_.4), channel_id=1, source_target_pairs={{0,4},{1,5},{2,6},{3,7},{4,0},{5,1},{6,2},{7,3},{8,12},{9,13},{10,... | collective-permute-start | bytes 786440 | tf_op jit(solution)/shard_map/ppermute | solution.py:514
  5.2 1.6 %collective-permute-start.3 = (bf16[512,256]{1,0:T(8,128)(2,1)}, bf16[512,256]{1,0:T(8,128)(2,1)S(1)}, u32[]{:S(2)}, u32[]{:S(2)}) collective-permute-start(bf16[512,256]{1,0:T(8,128)(2,1)} %refs_8_.4), channel_id=1, source_target_pairs={{0,8},{1,9},{2,10},{3,11},{4,12},{5,13},{6,14},{7,15},{8,16},{9,17... | collective-permute-start | bytes 786440 | tf_op jit(solution)/shard_map/ppermute | solution.py:514
  6.7 1.6 %collective-permute-start.4 = (bf16[512,256]{1,0:T(8,128)(2,1)}, bf16[512,256]{1,0:T(8,128)(2,1)S(1)}, u32[]{:S(2)}, u32[]{:S(2)}) collective-permute-start(bf16[512,256]{1,0:T(8,128)(2,1)} %refs_10_.1), channel_id=1, source_target_pairs={{0,8},{1,9},{2,10},{3,11},{4,12},{5,13},{6,14},{7,15},{8,16},{9,17... | collective-permute-start | bytes 786440 | tf_op jit(solution)/shard_map/ppermute | solution.py:514
  8.3 0.7 dynamic-slice_bitcast_fusion
  9.1 0.2 reduce-window.4
  9.2 0.7 fusion.24
  10.0 0.1 iota_compare_fusion.2
  10.0 0.7 pad_add_fusion
  10.7 0.1 select_reduce_fusion.1.refs_0_
  10.9 0.8 select_reduce_fusion
  11.6 0.5 fusion.1
  12.1 0.3 fusion.3
  12.4 0.4 fusion.28
  12.8 0.1 add_convert_fusion
  12.9 0.1 convert_element_type.52
  13.0 2.8 %collective-permute-done.1.refs_2_ = bf16[64,4096]{1,0:T(8,128)(2,1)S(1)} collective-permute-done((bf16[64,4096]{1,0:T(8,128)(2,1)}, bf16[64,4096]{1,0:T(8,128)(2,1)S(1)}, u32[]{:S(2)}, u32[]{:S(2)}) %collective-permute-start.1) | collective-permute-done | bytes 524320 | tf_op jit(solution)/shard_map/ppermute | solution.py:514
  15.8 0.0 collective-permute-start.2
  15.8 0.5 fusion.17
  16.4 0.1 pad_maximum_fusion.refs_5_
  16.5 0.1 pad_maximum_fusion.1.refs_6_
  16.6 0.0 collective-permute-done.3.refs_3_
  16.6 1.8 %collective-permute-start.11 = (bf16[512,256]{1,0:T(8,128)(2,1)}, bf16[512,256]{1,0:T(8,128)(2,1)S(1)}, u32[]{:S(2)}, u32[]{:S(2)}) collective-permute-start(bf16[512,256]{1,0:T(8,128)(2,1)} %refs_10_.1), channel_id=1, source_target_pairs={{0,4},{1,5},{2,6},{3,7},{4,0},{5,1},{6,2},{7,3},{8,12},{9,13},{10,... | collective-permute-start | bytes 786440 | tf_op jit(solution)/shard_map/ppermute | solution.py:514
  18.4 2.9 %collective-permute-done.4.refs_6_ = bf16[512,256]{1,0:T(8,128)(2,1)S(1)} collective-permute-done((bf16[512,256]{1,0:T(8,128)(2,1)}, bf16[512,256]{1,0:T(8,128)(2,1)S(1)}, u32[]{:S(2)}, u32[]{:S(2)}) %collective-permute-start.4) | collective-permute-done | bytes 262176 | tf_op jit(solution)/shard_map/ppermute | solution.py:514
  21.3 0.6 collective-permute-start.15
  21.9 0.0 collective-permute-done.2.refs_3_
  21.9 1.2 %collective-permute-start.6 = (bf16[512,256]{1,0:T(8,128)(2,1)S(1)}, bf16[512,256]{1,0:T(8,128)(2,1)S(1)}, u32[]{:S(2)}, u32[]{:S(2)}) collective-permute-start(bf16[512,256]{1,0:T(8,128)(2,1)S(1)} %collective-permute-done.4.refs_6_), channel_id=1, source_target_pairs={{0,8},{1,9},{2,10},{3,11},{4,12},{5,13},{6,14},{7,15},{8,16},{9,17... | collective-permute-start | bytes 786440 | tf_op jit(solution)/shard_map/ppermute | solution.py:514
  23.1 1.0 %copy-done.15 = bf16[64,4096]{1,0:T(8,128)(2,1)S(1)} copy-done((bf16[64,4096]{1,0:T(8,128)(2,1)S(1)}, bf16[64,4096]{1,0:T(8,128)(2,1)}, u32[]{:S(2)}) %copy-start.15) | copy-done | bytes 524312
  24.2 0.7 copy-done.26
  24.9 6.0 %project.1 = (bf16[4,8,64,128]{3,2,1,0:T(8,128)(2,1)S(1)}, bf16[256,256]{1,0:T(8,128)(2,1)S(1)}, bf16[256,256]{1,0:T(8,128)(2,1)S(1)}) custom-call(bf16[64,4096]{1,0:T(8,128)(2,1)S(1)} %copy-done.15, bf16[64,4096]{1,0:T(8,128)(2,1)S(1)} %collective-permute-done.refs_1_, bf16[64,4096]{1,0:T(8,128)(2,1)S(1)} %collective-permute-done.1.refs_2_, ...), custom_call_target="tpu_custom_call" | custom-call | flops 7699999744 | tf_op jit(solution)/shard_map/project/pallas_call | solution.py:27
  31.0 0.0 copy-start.3
  31.0 1.4 %collective-permute-done.5.refs_5_ = bf16[512,256]{1,0:T(8,128)(2,1)S(1)} collective-permute-done((bf16[512,256]{1,0:T(8,128)(2,1)S(1)}, bf16[512,256]{1,0:T(8,128)(2,1)S(1)}, u32[]{:S(2)}, u32[]{:S(2)}) %collective-permute-start.5) | collective-permute-done | bytes 262176 | tf_op jit(solution)/shard_map/ppermute | solution.py:514
  32.4 0.5 collective-permute-start.16
  32.9 3.6 %collective-permute-done.6.refs_8_ = bf16[512,256]{1,0:T(8,128)(2,1)S(1)} collective-permute-done((bf16[512,256]{1,0:T(8,128)(2,1)S(1)}, bf16[512,256]{1,0:T(8,128)(2,1)S(1)}, u32[]{:S(2)}, u32[]{:S(2)}) %collective-permute-start.6) | collective-permute-done | bytes 262176 | tf_op jit(solution)/shard_map/ppermute | solution.py:514
  36.5 0.5 collective-permute-start.13
  37.0 0.0 collective-permute-done.10.refs_9_
  37.0 0.1 collective-permute-start.8
  37.1 9.4 %attend_first.1 = (f32[4,2,256,128]{3,2,1,0:T(8,128)S(1)}, f32[4,2,256,128]{3,2,1,0:T(8,128)S(1)}, f32[4,2,256,128]{3,2,1,0:T(8,128)S(1)}) custom-call(s32[3,4]{1,0:T(4,128)S(1)} %select_reduce_fusion.1.refs_0_, s32[8]{0:T(128)S(1)} %fusion.20.refs_1_, bf16[4,8,64,128]{3,2,1,0:T(8,128)(2,1)S(1)} %get-tuple-element.27.refs_2_, ...), custom_call_target="tpu_custom_call" | custom-call | flops 6600000000 | tf_op jit(solution)/shard_map/attend_first/pallas_call | solution.py:27
  46.6 4.4 %collective-permute-done.8.refs_4_ = bf16[512,256]{1,0:T(8,128)(2,1)S(1)} collective-permute-done((bf16[512,256]{1,0:T(8,128)(2,1)S(1)}, bf16[512,256]{1,0:T(8,128)(2,1)S(1)}, u32[]{:S(2)}, u32[]{:S(2)}) %collective-permute-start.8) | collective-permute-done | bytes 262176 | tf_op jit(solution)/shard_map/ppermute | solution.py:514
  50.9 1.5 %collective-permute-start.7 = (bf16[512,256]{1,0:T(8,128)(2,1)S(1)}, bf16[512,256]{1,0:T(8,128)(2,1)S(1)}, u32[]{:S(2)}, u32[]{:S(2)}) collective-permute-start(bf16[512,256]{1,0:T(8,128)(2,1)S(1)} %collective-permute-done.5.refs_5_), channel_id=1, source_target_pairs={{0,4},{1,5},{2,6},{3,7},{4,0},{5,1},{6,2},{7,3},{8,12},{9,13},{10,... | collective-permute-start | bytes 786440 | tf_op jit(solution)/shard_map/ppermute | solution.py:514
  52.4 0.5 collective-permute-start.12
  53.0 0.0 collective-permute-start.14
  53.0 3.4 %attend_middle.2 = (f32[4,2,256,128]{3,2,1,0:T(8,128)S(1)}, f32[4,2,256,128]{3,2,1,0:T(8,128)S(1)}, f32[4,2,256,128]{3,2,1,0:T(8,128)S(1)}) custom-call(s32[3,4]{1,0:T(4,128)S(1)} %select_reduce_fusion.1.refs_0_, s32[8]{0:T(128)S(1)} %fusion.20.refs_1_, bf16[4,8,64,128]{3,2,1,0:T(8,128)(2,1)S(1)} %get-tuple-element.27.refs_2_, ...), custom_call_target="tpu_custom_call" | custom-call | flops 2969999872 | tf_op jit(solution)/shard_map/attend_middle/pallas_call | solution.py:27
  56.5 2.9 %collective-permute-done.7.refs_3_ = bf16[512,256]{1,0:T(8,128)(2,1)S(1)} collective-permute-done((bf16[512,256]{1,0:T(8,128)(2,1)S(1)}, bf16[512,256]{1,0:T(8,128)(2,1)S(1)}, u32[]{:S(2)}, u32[]{:S(2)}) %collective-permute-start.7) | collective-permute-done | bytes 262176 | tf_op jit(solution)/shard_map/ppermute | solution.py:514
  59.4 3.0 %attend_middle.3 = (f32[2,2,256,128]{3,2,1,0:T(8,128)S(1)}, f32[2,2,256,128]{3,2,1,0:T(8,128)S(1)}, f32[2,2,256,128]{3,2,1,0:T(8,128)S(1)}) custom-call(s32[3,4]{1,0:T(4,128)S(1)} %select_reduce_fusion.1.refs_0_, s32[8]{0:T(128)S(1)} %fusion.20.refs_1_, bf16[4,8,64,128]{3,2,1,0:T(8,128)(2,1)S(1)} %get-tuple-element.27.refs_2_, ...), custom_call_target="tpu_custom_call" | custom-call | flops 1210000000 | tf_op jit(solution)/shard_map/attend_middle/pallas_call | solution.py:27
  62.5 0.0 copy-start.29
  62.5 4.6 %attend_last.2 = (bf16[64,4096]{1,0:T(8,128)(2,1)S(1)}, bf16[64,4096]{1,0:T(8,128)(2,1)S(1)}) custom-call(s32[3,4]{1,0:T(4,128)S(1)} %select_reduce_fusion.1.refs_0_, s32[8]{0:T(128)S(1)} %fusion.20.refs_1_, bf16[4,8,64,128]{3,2,1,0:T(8,128)(2,1)S(1)} %get-tuple-element.27.refs_2_, bf16[512,256]{1,0:T(8,128)(2,1)S(1)} %collective-permute-done.12.refs_3_.refs_5_, ...), custom_call_target="tpu_custom_call" | custom-call | flops 4729999872 | tf_op jit(solution)/shard_map/attend_last/pallas_call | solution.py:27
  67.1 0.0 copy-start.4
  67.2 0.1 collective-permute-start.17
  67.3 0.1 broadcast_add_fusion
  67.3 0.1 reshape.130
  67.4 1.7 %collective-permute-done.17.refs_1_ = bf16[64,4096]{1,0:T(8,128)(2,1)S(1)} collective-permute-done((bf16[64,4096]{1,0:T(8,128)(2,1)S(1)}, bf16[64,4096]{1,0:T(8,128)(2,1)S(1)}, u32[]{:S(2)}, u32[]{:S(2)}) %collective-permute-start.17) | collective-permute-done | bytes 524320 | tf_op jit(solution)/shard_map/ppermute | solution.py:514
  69.1 0.1 add_up.3.refs_13_
  69.3 1.3 %collective-permute-start.18 = (bf16[64,4096]{1,0:T(8,128)(2,1)S(1)}, bf16[64,4096]{1,0:T(8,128)(2,1)S(1)}, u32[]{:S(2)}, u32[]{:S(2)}) collective-permute-start(bf16[64,4096]{1,0:T(8,128)(2,1)S(1)} %add_up.3.refs_13_), channel_id=1, source_target_pairs={{0,2},{1,3},{2,0},{3,1},{4,6},{5,7},{6,4},{7,5},{8,10},{9,11},{10,... | collective-permute-start | bytes 1572872 | tf_op jit(solution)/shard_map/ppermute | solution.py:514
  70.6 7.3 %attend_last.3 = (bf16[64,4096]{1,0:T(8,128)(2,1)S(1)}, bf16[64,4096]{1,0:T(8,128)(2,1)S(1)}) custom-call(s32[3,4]{1,0:T(4,128)S(1)} %select_reduce_fusion.1.refs_0_, s32[8]{0:T(128)S(1)} %fusion.20.refs_1_, bf16[4,8,64,128]{3,2,1,0:T(8,128)(2,1)S(1)} %copy-done.4, bf16[512,256]{1,0:T(8,128)(2,1)S(1)} %copy-done.10, bf16[512,256]{1,0:T(8,128)(2,1)S(1)} %copy-done.8, ...), custom_call_target="tpu_custom_call" | custom-call | flops 6489999872 | tf_op jit(solution)/shard_map/attend_last/pallas_call | solution.py:27
  77.9 0.0 copy-start.27
  77.9 0.8 copy-done.27
  78.7 0.6 gather_fusion
  79.3 0.6 gather_fusion.1
  79.9 0.7 select_bitcast_fusion
  80.6 2.7 %collective-permute-done.18.refs_1_ = bf16[64,4096]{1,0:T(8,128)(2,1)S(1)} collective-permute-done((bf16[64,4096]{1,0:T(8,128)(2,1)S(1)}, bf16[64,4096]{1,0:T(8,128)(2,1)S(1)}, u32[]{:S(2)}, u32[]{:S(2)}) %collective-permute-start.18) | collective-permute-done | bytes 524320 | tf_op jit(solution)/shard_map/ppermute | solution.py:514
  83.3 1.0 %copy-done.28 = bf16[64,4096]{1,0:T(8,128)(2,1)S(1)} copy-done((bf16[64,4096]{1,0:T(8,128)(2,1)S(1)}, bf16[64,4096]{1,0:T(8,128)(2,1)}, u32[]{:S(2)}) %copy-start.28) | copy-done | bytes 524312
  84.3 0.1 add_up.4.refs_0_
  84.5 0.9 %add_up.5 = bf16[64,4096]{1,0:T(8,128)(2,1)} custom-call(f32[64,4096]{1,0:T(8,128)S(1)} %add_up.4.refs_0_, bf16[64,4096]{1,0:T(8,128)(2,1)S(1)} %collective-permute-done.19.refs_1_), custom_call_target="tpu_custom_call" | custom-call | flops 1100000000 | tf_op jit(solution)/shard_map/add_up/pallas_call | solution.py:27
  (74 shorter events, 0.2 us)
Async XLA Ops:
  0.6 15.2 %collective-permute-start.1 = (bf16[64,4096]{1,0:T(8,128)(2,1)}, bf16[64,4096]{1,0:T(8,128)(2,1)S(1)}, u32[]{:S(2)}, u32[]{:S(2)}) collective-permute-start(bf16[64,4096]{1,0:T(8,128)(2,1)} %refs_0_.1), channel_id=1, source_target_pairs={{0,2},{1,3},{2,0},{3,1},{4,6},{5,7},{6,4},{7,5},{8,10},{9,11},{10,... | collective-permute-start | bytes 1572872 | tf_op jit(solution)/shard_map/ppermute | solution.py:514
  3.7 17.7 %collective-permute-start = (bf16[64,4096]{1,0:T(8,128)(2,1)}, bf16[64,4096]{1,0:T(8,128)(2,1)S(1)}, u32[]{:S(2)}, u32[]{:S(2)}) collective-permute-start(bf16[64,4096]{1,0:T(8,128)(2,1)} %refs_0_.1), channel_id=1, source_target_pairs={{0,1},{1,0},{2,3},{3,2},{4,5},{5,4},{6,7},{7,6},{8,9},{9,8},{10,11... | collective-permute-start | bytes 1572872 | tf_op jit(solution)/shard_map/ppermute | solution.py:514
  3.7 33.3 %collective-permute-start.10 = (bf16[512,256]{1,0:T(8,128)(2,1)}, bf16[512,256]{1,0:T(8,128)(2,1)S(1)}, u32[]{:S(2)}, u32[]{:S(2)}) collective-permute-start(bf16[512,256]{1,0:T(8,128)(2,1)} %refs_8_.4), channel_id=1, source_target_pairs={{0,4},{1,5},{2,6},{3,7},{4,0},{5,1},{6,2},{7,3},{8,12},{9,13},{10,... | collective-permute-start | bytes 786440 | tf_op jit(solution)/shard_map/ppermute | solution.py:514
  5.2 11.4 %collective-permute-start.3 = (bf16[512,256]{1,0:T(8,128)(2,1)}, bf16[512,256]{1,0:T(8,128)(2,1)S(1)}, u32[]{:S(2)}, u32[]{:S(2)}) collective-permute-start(bf16[512,256]{1,0:T(8,128)(2,1)} %refs_8_.4), channel_id=1, source_target_pairs={{0,8},{1,9},{2,10},{3,11},{4,12},{5,13},{6,14},{7,15},{8,16},{9,17... | collective-permute-start | bytes 786440 | tf_op jit(solution)/shard_map/ppermute | solution.py:514
  6.7 14.6 %collective-permute-start.4 = (bf16[512,256]{1,0:T(8,128)(2,1)}, bf16[512,256]{1,0:T(8,128)(2,1)S(1)}, u32[]{:S(2)}, u32[]{:S(2)}) collective-permute-start(bf16[512,256]{1,0:T(8,128)(2,1)} %refs_10_.1), channel_id=1, source_target_pairs={{0,8},{1,9},{2,10},{3,11},{4,12},{5,13},{6,14},{7,15},{8,16},{9,17... | collective-permute-start | bytes 786440 | tf_op jit(solution)/shard_map/ppermute | solution.py:514
  15.8 6.1 %collective-permute-start.2 = (bf16[64,4096]{1,0:T(8,128)(2,1)S(1)}, bf16[64,4096]{1,0:T(8,128)(2,1)S(1)}, u32[]{:S(2)}, u32[]{:S(2)}) collective-permute-start(bf16[64,4096]{1,0:T(8,128)(2,1)S(1)} %collective-permute-done.1.refs_2_), channel_id=1, source_target_pairs={{0,1},{1,0},{2,3},{3,2},{4,5},{5,4},{6,7},{7,6},{8,9},{9,8},{10,11... | collective-permute-start | bytes 1572872 | tf_op jit(solution)/shard_map/ppermute | solution.py:514
  16.6 14.3 %copy-start.18 = (bf16[512,256]{1,0:T(8,128)(2,1)}, bf16[512,256]{1,0:T(8,128)(2,1)S(1)}, u32[]{:S(2)}) copy-start(bf16[512,256]{1,0:T(8,128)(2,1)S(1)} %collective-permute-done.3.refs_3_) | copy-start | bytes 786436
  16.6 20.4 %collective-permute-start.11 = (bf16[512,256]{1,0:T(8,128)(2,1)}, bf16[512,256]{1,0:T(8,128)(2,1)S(1)}, u32[]{:S(2)}, u32[]{:S(2)}) collective-permute-start(bf16[512,256]{1,0:T(8,128)(2,1)} %refs_10_.1), channel_id=1, source_target_pairs={{0,4},{1,5},{2,6},{3,7},{4,0},{5,1},{6,2},{7,3},{8,12},{9,13},{10,... | collective-permute-start | bytes 786440 | tf_op jit(solution)/shard_map/ppermute | solution.py:514
  21.3 11.0 %copy-start.20 = (bf16[512,256]{1,0:T(8,128)(2,1)}, bf16[512,256]{1,0:T(8,128)(2,1)S(1)}, u32[]{:S(2)}) copy-start(bf16[512,256]{1,0:T(8,128)(2,1)S(1)} %collective-permute-done.4.refs_6_) | copy-start | bytes 786436
  21.3 11.0 %collective-permute-start.5 = (bf16[512,256]{1,0:T(8,128)(2,1)S(1)}, bf16[512,256]{1,0:T(8,128)(2,1)S(1)}, u32[]{:S(2)}, u32[]{:S(2)}) collective-permute-start(bf16[512,256]{1,0:T(8,128)(2,1)S(1)} %collective-permute-done.3.refs_3_), channel_id=1, source_target_pairs={{0,8},{1,9},{2,10},{3,11},{4,12},{5,13},{6,14},{7,15},{8,16},{9,17... | collective-permute-start | bytes 786440 | tf_op jit(solution)/shard_map/ppermute | solution.py:514
  21.3 31.7 %collective-permute-start.15 = (bf16[512,256]{1,0:T(8,128)(2,1)S(1)}, bf16[512,256]{1,0:T(8,128)(2,1)S(1)}, u32[]{:S(2)}, u32[]{:S(2)}) collective-permute-start(bf16[512,256]{1,0:T(8,128)(2,1)S(1)} %collective-permute-done.3.refs_3_), channel_id=1, source_target_pairs={{0,4},{1,5},{2,6},{3,7},{4,0},{5,1},{6,2},{7,3},{8,12},{9,13},{10,... | collective-permute-start | bytes 786440 | tf_op jit(solution)/shard_map/ppermute | solution.py:514
  21.9 14.5 %collective-permute-start.6 = (bf16[512,256]{1,0:T(8,128)(2,1)S(1)}, bf16[512,256]{1,0:T(8,128)(2,1)S(1)}, u32[]{:S(2)}, u32[]{:S(2)}) collective-permute-start(bf16[512,256]{1,0:T(8,128)(2,1)S(1)} %collective-permute-done.4.refs_6_), channel_id=1, source_target_pairs={{0,8},{1,9},{2,10},{3,11},{4,12},{5,13},{6,14},{7,15},{8,16},{9,17... | collective-permute-start | bytes 786440 | tf_op jit(solution)/shard_map/ppermute | solution.py:514
  23.1 1.0 %copy-start.15 = (bf16[64,4096]{1,0:T(8,128)(2,1)S(1)}, bf16[64,4096]{1,0:T(8,128)(2,1)}, u32[]{:S(2)}) copy-start(bf16[64,4096]{1,0:T(8,128)(2,1)} %refs_0_.1) | copy-start | bytes 1572868
  24.2 0.7 copy-start.26
  24.9 12.2 %copy-start.13 = (bf16[4608,256]{1,0:T(8,128)(2,1)S(1)}, bf16[4608,256]{1,0:T(8,128)(2,1)}, u32[]{:S(2)}) copy-start(bf16[4608,256]{1,0:T(8,128)(2,1)} %refs_6_.1) | copy-start | bytes 7077892
  24.9 12.2 %copy-start.14 = (bf16[4608,256]{1,0:T(8,128)(2,1)S(1)}, bf16[4608,256]{1,0:T(8,128)(2,1)}, u32[]{:S(2)}) copy-start(bf16[4608,256]{1,0:T(8,128)(2,1)} %refs_7_.3) | copy-start | bytes 7077892
  24.9 12.2 %copy-start.16 = (bf16[512,256]{1,0:T(8,128)(2,1)S(1)}, bf16[512,256]{1,0:T(8,128)(2,1)}, u32[]{:S(2)}) copy-start(bf16[512,256]{1,0:T(8,128)(2,1)} %refs_8_.4) | copy-start | bytes 786436
  24.9 12.2 %copy-start.17 = (bf16[512,256]{1,0:T(8,128)(2,1)S(1)}, bf16[512,256]{1,0:T(8,128)(2,1)}, u32[]{:S(2)}) copy-start(bf16[512,256]{1,0:T(8,128)(2,1)} %refs_10_.1) | copy-start | bytes 786436
  31.0 15.6 %copy-start.11 = (bf16[256,256]{1,0:T(8,128)(2,1)}, bf16[256,256]{1,0:T(8,128)(2,1)S(1)}, u32[]{:S(2)}) copy-start(bf16[256,256]{1,0:T(8,128)(2,1)S(1)} %get-tuple-element.34.refs_3_) | copy-start | bytes 393220
  31.0 31.5 %copy-start.3 = (bf16[4,8,64,128]{3,2,1,0:T(8,128)(2,1)}, bf16[4,8,64,128]{3,2,1,0:T(8,128)(2,1)S(1)}, u32[]{:S(2)}) copy-start(bf16[4,8,64,128]{3,2,1,0:T(8,128)(2,1)S(1)} %get-tuple-element.27.refs_2_) | copy-start | bytes 1572868
  32.4 20.6 %collective-permute-start.16 = (bf16[512,256]{1,0:T(8,128)(2,1)S(1)}, bf16[512,256]{1,0:T(8,128)(2,1)S(1)}, u32[]{:S(2)}, u32[]{:S(2)}) collective-permute-start(bf16[512,256]{1,0:T(8,128)(2,1)S(1)} %collective-permute-done.4.refs_6_), channel_id=1, source_target_pairs={{0,4},{1,5},{2,6},{3,7},{4,0},{5,1},{6,2},{7,3},{8,12},{9,13},{10,... | collective-permute-start | bytes 786440 | tf_op jit(solution)/shard_map/ppermute | solution.py:514
  36.5 16.5 %collective-permute-start.13 = (bf16[512,256]{1,0:T(8,128)(2,1)S(1)}, bf16[512,256]{1,0:T(8,128)(2,1)S(1)}, u32[]{:S(2)}, u32[]{:S(2)}) collective-permute-start(bf16[512,256]{1,0:T(8,128)(2,1)S(1)} %collective-permute-done.6.refs_8_), channel_id=1, source_target_pairs={{0,4},{1,5},{2,6},{3,7},{4,0},{5,1},{6,2},{7,3},{8,12},{9,13},{10,... | collective-permute-start | bytes 786440 | tf_op jit(solution)/shard_map/ppermute | solution.py:514
  37.0 15.4 %collective-permute-start.9 = (bf16[512,256]{1,0:T(8,128)(2,1)S(1)}, bf16[512,256]{1,0:T(8,128)(2,1)S(1)}, u32[]{:S(2)}, u32[]{:S(2)}) collective-permute-start(bf16[512,256]{1,0:T(8,128)(2,1)S(1)} %collective-permute-done.6.refs_8_), channel_id=1, source_target_pairs={{0,8},{1,9},{2,10},{3,11},{4,12},{5,13},{6,14},{7,15},{8,16},{9,17... | collective-permute-start | bytes 786440 | tf_op jit(solution)/shard_map/ppermute | solution.py:514
  37.0 13.9 %collective-permute-start.8 = (bf16[512,256]{1,0:T(8,128)(2,1)S(1)}, bf16[512,256]{1,0:T(8,128)(2,1)S(1)}, u32[]{:S(2)}, u32[]{:S(2)}) collective-permute-start(bf16[512,256]{1,0:T(8,128)(2,1)S(1)} %collective-permute-done.5.refs_5_), channel_id=1, source_target_pairs={{0,8},{1,9},{2,10},{3,11},{4,12},{5,13},{6,14},{7,15},{8,16},{9,17... | collective-permute-start | bytes 786440 | tf_op jit(solution)/shard_map/ppermute | solution.py:514
  37.1 15.9 %copy-start.19 = (bf16[512,256]{1,0:T(8,128)(2,1)S(1)}, bf16[512,256]{1,0:T(8,128)(2,1)}, u32[]{:S(2)}) copy-start(bf16[512,256]{1,0:T(8,128)(2,1)} %copy-done.18) | copy-start | bytes 786436
  37.1 15.9 %copy-start.21 = (bf16[512,256]{1,0:T(8,128)(2,1)S(1)}, bf16[512,256]{1,0:T(8,128)(2,1)}, u32[]{:S(2)}) copy-start(bf16[512,256]{1,0:T(8,128)(2,1)} %copy-done.20) | copy-start | bytes 786436
  50.9 8.4 %copy-start.7 = (bf16[512,256]{1,0:T(8,128)(2,1)}, bf16[512,256]{1,0:T(8,128)(2,1)S(1)}, u32[]{:S(2)}) copy-start(bf16[512,256]{1,0:T(8,128)(2,1)S(1)} %collective-permute-done.8.refs_4_) | copy-start | bytes 786436
  50.9 8.4 %collective-permute-start.7 = (bf16[512,256]{1,0:T(8,128)(2,1)S(1)}, bf16[512,256]{1,0:T(8,128)(2,1)S(1)}, u32[]{:S(2)}, u32[]{:S(2)}) collective-permute-start(bf16[512,256]{1,0:T(8,128)(2,1)S(1)} %collective-permute-done.5.refs_5_), channel_id=1, source_target_pairs={{0,4},{1,5},{2,6},{3,7},{4,0},{5,1},{6,2},{7,3},{8,12},{9,13},{10,... | collective-permute-start | bytes 786440 | tf_op jit(solution)/shard_map/ppermute | solution.py:514
  52.4 6.9 %copy-start.5 = (bf16[512,256]{1,0:T(8,128)(2,1)}, bf16[512,256]{1,0:T(8,128)(2,1)S(1)}, u32[]{:S(2)}) copy-start(bf16[512,256]{1,0:T(8,128)(2,1)S(1)} %collective-permute-done.9.refs_6_.refs_7_) | copy-start | bytes 786436
  52.4 10.0 %collective-permute-start.12 = (bf16[512,256]{1,0:T(8,128)(2,1)S(1)}, bf16[512,256]{1,0:T(8,128)(2,1)S(1)}, u32[]{:S(2)}, u32[]{:S(2)}) collective-permute-start(bf16[512,256]{1,0:T(8,128)(2,1)S(1)} %collective-permute-done.8.refs_4_), channel_id=1, source_target_pairs={{0,4},{1,5},{2,6},{3,7},{4,0},{5,1},{6,2},{7,3},{8,12},{9,13},{10,... | collective-permute-start | bytes 786440 | tf_op jit(solution)/shard_map/ppermute | solution.py:514
  53.0 9.5 %collective-permute-start.14 = (bf16[512,256]{1,0:T(8,128)(2,1)S(1)}, bf16[512,256]{1,0:T(8,128)(2,1)S(1)}, u32[]{:S(2)}, u32[]{:S(2)}) collective-permute-start(bf16[512,256]{1,0:T(8,128)(2,1)S(1)} %collective-permute-done.13.refs_5_.refs_6_), channel_id=1, source_target_pairs={{0,8},{1,9},{2,10},{3,11},{4,12},{5,13},{6,14},{7,15},{8,16},{9,17... | collective-permute-start | bytes 786440 | tf_op jit(solution)/shard_map/ppermute | solution.py:514
  56.4 6.0 %copy-start = (f32[4,2,256,128]{3,2,1,0:T(8,128)}, f32[4,2,256,128]{3,2,1,0:T(8,128)S(1)}, u32[]{:S(2)}) copy-start(f32[4,2,256,128]{3,2,1,0:T(8,128)S(1)} %get-tuple-element.40.refs_7_.refs_9_) | copy-start | bytes 3145732
  56.4 6.0 %copy-start.1 = (f32[4,2,256,128]{3,2,1,0:T(8,128)}, f32[4,2,256,128]{3,2,1,0:T(8,128)S(1)}, u32[]{:S(2)}) copy-start(f32[4,2,256,128]{3,2,1,0:T(8,128)S(1)} %get-tuple-element.41.refs_8_.refs_10_) | copy-start | bytes 3145732
  56.4 6.0 %copy-start.2 = (f32[4,2,256,128]{3,2,1,0:T(8,128)}, f32[4,2,256,128]{3,2,1,0:T(8,128)S(1)}, u32[]{:S(2)}) copy-start(f32[4,2,256,128]{3,2,1,0:T(8,128)S(1)} %get-tuple-element.42.refs_9_.refs_11_) | copy-start | bytes 3145732
  59.4 3.1 %copy-start.9 = (bf16[512,256]{1,0:T(8,128)(2,1)}, bf16[512,256]{1,0:T(8,128)(2,1)S(1)}, u32[]{:S(2)}) copy-start(bf16[512,256]{1,0:T(8,128)(2,1)S(1)} %collective-permute-done.7.refs_3_) | copy-start | bytes 786436
  62.4 4.7 %copy-start.22 = (bf16[512,256]{1,0:T(8,128)(2,1)}, bf16[512,256]{1,0:T(8,128)(2,1)S(1)}, u32[]{:S(2)}) copy-start(bf16[512,256]{1,0:T(8,128)(2,1)S(1)} %collective-permute-done.12.refs_3_.refs_5_) | copy-start | bytes 786436
  62.5 4.7 %copy-start.24 = (bf16[512,256]{1,0:T(8,128)(2,1)}, bf16[512,256]{1,0:T(8,128)(2,1)S(1)}, u32[]{:S(2)}) copy-start(bf16[512,256]{1,0:T(8,128)(2,1)S(1)} %collective-permute-done.14.refs_4_.refs_8_) | copy-start | bytes 786436
  62.5 4.8 %copy-start.29 = (s32[4,8]{1,0:T(4,128)S(1)}, s32[4,8]{1,0:T(4,128)}, u32[]{:S(2)}) copy-start(s32[4,8]{1,0:T(4,128)} %param.29) | copy-start | bytes 388
  67.1 3.4 %copy-start.4 = (bf16[4,8,64,128]{3,2,1,0:T(8,128)(2,1)S(1)}, bf16[4,8,64,128]{3,2,1,0:T(8,128)(2,1)}, u32[]{:S(2)}) copy-start(bf16[4,8,64,128]{3,2,1,0:T(8,128)(2,1)} %copy-done.3) | copy-start | bytes 1572868
  67.1 3.4 %copy-start.6 = (bf16[512,256]{1,0:T(8,128)(2,1)S(1)}, bf16[512,256]{1,0:T(8,128)(2,1)}, u32[]{:S(2)}) copy-start(bf16[512,256]{1,0:T(8,128)(2,1)} %copy-done.5) | copy-start | bytes 786436
  67.1 3.4 %copy-start.8 = (bf16[512,256]{1,0:T(8,128)(2,1)S(1)}, bf16[512,256]{1,0:T(8,128)(2,1)}, u32[]{:S(2)}) copy-start(bf16[512,256]{1,0:T(8,128)(2,1)} %copy-done.7) | copy-start | bytes 786436
  67.2 3.4 %copy-start.10 = (bf16[512,256]{1,0:T(8,128)(2,1)S(1)}, bf16[512,256]{1,0:T(8,128)(2,1)}, u32[]{:S(2)}) copy-start(bf16[512,256]{1,0:T(8,128)(2,1)} %copy-done.9) | copy-start | bytes 786436
  67.2 2.0 %collective-permute-start.17 = (bf16[64,4096]{1,0:T(8,128)(2,1)S(1)}, bf16[64,4096]{1,0:T(8,128)(2,1)S(1)}, u32[]{:S(2)}, u32[]{:S(2)}) collective-permute-start(bf16[64,4096]{1,0:T(8,128)(2,1)S(1)} %get-tuple-element.47), channel_id=1, source_target_pairs={{0,1},{1,0},{2,3},{3,2},{4,5},{5,4},{6,7},{7,6},{8,9},{9,8},{10,11... | collective-permute-start | bytes 1572872 | tf_op jit(solution)/shard_map/ppermute | solution.py:514
  67.4 3.1 %copy-start.23 = (bf16[512,256]{1,0:T(8,128)(2,1)S(1)}, bf16[512,256]{1,0:T(8,128)(2,1)}, u32[]{:S(2)}) copy-start(bf16[512,256]{1,0:T(8,128)(2,1)} %copy-done.22) | copy-start | bytes 786436
  67.4 3.1 %copy-start.25 = (bf16[512,256]{1,0:T(8,128)(2,1)S(1)}, bf16[512,256]{1,0:T(8,128)(2,1)}, u32[]{:S(2)}) copy-start(bf16[512,256]{1,0:T(8,128)(2,1)} %copy-done.24) | copy-start | bytes 786436
  69.3 9.4 %copy-start.12 = (bf16[256,256]{1,0:T(8,128)(2,1)S(1)}, bf16[256,256]{1,0:T(8,128)(2,1)}, u32[]{:S(2)}) copy-start(bf16[256,256]{1,0:T(8,128)(2,1)} %copy-done.11) | copy-start | bytes 393220
  69.3 14.0 %collective-permute-start.18 = (bf16[64,4096]{1,0:T(8,128)(2,1)S(1)}, bf16[64,4096]{1,0:T(8,128)(2,1)S(1)}, u32[]{:S(2)}, u32[]{:S(2)}) collective-permute-start(bf16[64,4096]{1,0:T(8,128)(2,1)S(1)} %add_up.3.refs_13_), channel_id=1, source_target_pairs={{0,2},{1,3},{2,0},{3,1},{4,6},{5,7},{6,4},{7,5},{8,10},{9,11},{10,... | collective-permute-start | bytes 1572872 | tf_op jit(solution)/shard_map/ppermute | solution.py:514
  77.9 0.8 copy-start.27
  78.7 5.8 %collective-permute-start.19 = (bf16[64,4096]{1,0:T(8,128)(2,1)S(1)}, bf16[64,4096]{1,0:T(8,128)(2,1)S(1)}, u32[]{:S(2)}, u32[]{:S(2)}) collective-permute-start(bf16[64,4096]{1,0:T(8,128)(2,1)S(1)} %get-tuple-element.49), channel_id=1, source_target_pairs={{0,1},{1,0},{2,3},{3,2},{4,5},{5,4},{6,7},{7,6},{8,9},{9,8},{10,11... | collective-permute-start | bytes 1572872 | tf_op jit(solution)/shard_map/ppermute | solution.py:514
  83.3 1.0 %copy-start.28 = (bf16[64,4096]{1,0:T(8,128)(2,1)S(1)}, bf16[64,4096]{1,0:T(8,128)(2,1)}, u32[]{:S(2)}) copy-start(bf16[64,4096]{1,0:T(8,128)(2,1)} %copy-done.27) | copy-start | bytes 1572868
where the time goes:
time: 85.7 us; the launch traced here: 85.4 us
  Pallas kernels  34.9 us (41%)
  waiting for transfers between devices  22.4 us (26%)
  starting transfers between devices  15.7 us (18%)
  local copies, waits for them, and re-layouts  5.86 us (7%)
  other arithmetic  4.2 us (5%)
  matrix products  1.15 us (1%)
  between operations  1.14 us (1%)
    pallas_call x9, Pallas kernels, call(): pl.pallas_call(wrapped, in_specs=in_specs + [HBM] * len(after), out_specs...  34.9 us
    ppermute x20, waiting for transfers between devices, body(): send = lambda a, p: lax.ppermute(a, AXES, p)  22.4 us
    ppermute x20, starting transfers between devices, body(): send = lambda a, p: lax.ppermute(a, AXES, p)  15.7 us
    unnamed x60, local copies, waits for them, and re-layouts  3.7 us
  transfers between devices with their start and end apart: 20, of which 8 were waited for; matrix products, arithmetic and copies ran while one was open for 9% of the time, Pallas kernels for 34%

commit v1 on v0

--- a/solution.py
+++ b/solution.py
@@ -347,7 +347,7 @@
     lax.fori_loop(0, reqs, one_request, 0)
 
 
-def attend_middle(queries, info, bases, shards, span, state, offset, reqs):
+def attend_middle(queries, info, bases, shards, span, state, offset, reqs, microseconds=0.3):
     shards = shards[span[0] : span[1]]
     _, n_heads, tree, _ = queries.shape
     kv_local = shards[0][0].shape[1] // HD
@@ -359,7 +359,7 @@
         state_shapes(reqs, kv_local, n_heads // kv_local * tree),
         shard_scratch(shards),
         40,
-        0.3 + 0.2 * n * reqs,
+        microseconds,
         "attend_middle",
     )
 
@@ -573,7 +573,7 @@
         shards += [ring[-1], side[-1]]
         n = len(shards)
         state = attend_middle(queries, info, bases, shards, (2, 5), state, 0, reqs)
-        far_state = attend_middle(queries, info, bases, shards, (5, n - 1), state, 2, 2)
+        far_state = attend_middle(queries, info, bases, shards, (5, n - 1), state, 2, 2, 4)
         final = functools.partial(attend_last, queries, info, bases, shards, w_out=w_out, reqs=2)
         kept, away = final((n - 1, n), far_state, offset=2)
         got = send(away, core_pairs)

time: 85.7 us -> 87.1 us (1.016)
  starting transfers between devices: 15.7 us -> 17.2 us
    ppermute x20, starting transfers between devices: 15.7 us -> 17.2 us  [body(): send = lambda a, p: lax.ppermute(a, AXES, p)]
    unnamed x60 -> x48, local copies, waits for them, and re-layouts: 3.7 us -> 3.67 us
  transfers between devices with their start and end apart: 20 -> 20, of which waited for: 8 -> 9; matrix products, arithmetic and copies ran while one was open for 9% -> 9% of each run, Pallas kernels for 34% -> 34%
where the time goes in v1:
time: 87.1 us; the launch traced here: 86.5 us
  Pallas kernels  34.9 us (40%)
  waiting for transfers between devices  22.1 us (25%)
  starting transfers between devices  17.2 us (20%)
  local copies, waits for them, and re-layouts  5.83 us (7%)
  other arithmetic  4.2 us (5%)
  matrix products  1.15 us (1%)
  between operations  1.03 us (1%)
    pallas_call x9, Pallas kernels, call(): pl.pallas_call(wrapped, in_specs=in_specs + [HBM] * len(after), out_specs...  34.9 us
    ppermute x20, waiting for transfers between devices, body(): send = lambda a, p: lax.ppermute(a, AXES, p)  22.1 us
    ppermute x20, starting transfers between devices, body(): send = lambda a, p: lax.ppermute(a, AXES, p)  17.2 us
    unnamed x48, local copies, waits for them, and re-layouts  3.67 us
  transfers between devices with their start and end apart: 20, of which 9 were waited for; matrix products, arithmetic and copies ran while one was open for 9% of the time, Pallas kernels for 34%

profile of v1, /device:TPU:0, one launch (start us, length us, event | category | flops | bytes accessed | tf_op | source)
XLA Modules:
  0.0 86.5 jit_solution(1220541082165793840)
XLA Ops:
  0.6 3.0 %collective-permute-start.1 = (bf16[64,4096]{1,0:T(8,128)(2,1)}, bf16[64,4096]{1,0:T(8,128)(2,1)S(1)}, u32[]{:S(2)}, u32[]{:S(2)}) collective-permute-start(bf16[64,4096]{1,0:T(8,128)(2,1)} %refs_0_.1), channel_id=1, source_target_pairs={{0,2},{1,3},{2,0},{3,1},{4,6},{5,7},{6,4},{7,5},{8,10},{9,11},{10,... | collective-permute-start | bytes 1572872 | tf_op jit(solution)/shard_map/ppermute | solution.py:514
  3.7 1.5 %collective-permute-start.10 = (bf16[512,256]{1,0:T(8,128)(2,1)}, bf16[512,256]{1,0:T(8,128)(2,1)S(1)}, u32[]{:S(2)}, u32[]{:S(2)}) collective-permute-start(bf16[512,256]{1,0:T(8,128)(2,1)} %refs_8_.4), channel_id=1, source_target_pairs={{0,4},{1,5},{2,6},{3,7},{4,0},{5,1},{6,2},{7,3},{8,12},{9,13},{10,... | collective-permute-start | bytes 786440 | tf_op jit(solution)/shard_map/ppermute | solution.py:514
  5.2 1.6 %collective-permute-start.3 = (bf16[512,256]{1,0:T(8,128)(2,1)}, bf16[512,256]{1,0:T(8,128)(2,1)S(1)}, u32[]{:S(2)}, u32[]{:S(2)}) collective-permute-start(bf16[512,256]{1,0:T(8,128)(2,1)} %refs_8_.4), channel_id=1, source_target_pairs={{0,8},{1,9},{2,10},{3,11},{4,12},{5,13},{6,14},{7,15},{8,16},{9,17... | collective-permute-start | bytes 786440 | tf_op jit(solution)/shard_map/ppermute | solution.py:514
  6.7 1.6 %collective-permute-start.4 = (bf16[512,256]{1,0:T(8,128)(2,1)}, bf16[512,256]{1,0:T(8,128)(2,1)S(1)}, u32[]{:S(2)}, u32[]{:S(2)}) collective-permute-start(bf16[512,256]{1,0:T(8,128)(2,1)} %refs_10_.1), channel_id=1, source_target_pairs={{0,8},{1,9},{2,10},{3,11},{4,12},{5,13},{6,14},{7,15},{8,16},{9,17... | collective-permute-start | bytes 786440 | tf_op jit(solution)/shard_map/ppermute | solution.py:514
  8.3 0.7 dynamic-slice_bitcast_fusion
  9.1 0.2 reduce-window.4
  9.2 0.7 fusion.24
  10.0 0.1 iota_compare_fusion.2
  10.0 0.7 pad_add_fusion
  10.7 0.1 select_reduce_fusion.1.refs_0_
  10.9 0.8 select_reduce_fusion
  11.6 0.5 fusion.1
  12.1 0.3 fusion.3
  12.4 0.4 fusion.28
  12.8 0.1 add_convert_fusion
  12.9 0.1 convert_element_type.52
  13.0 2.8 %collective-permute-done.1.refs_2_ = bf16[64,4096]{1,0:T(8,128)(2,1)S(1)} collective-permute-done((bf16[64,4096]{1,0:T(8,128)(2,1)}, bf16[64,4096]{1,0:T(8,128)(2,1)S(1)}, u32[]{:S(2)}, u32[]{:S(2)}) %collective-permute-start.1) | collective-permute-done | bytes 524320 | tf_op jit(solution)/shard_map/ppermute | solution.py:514
  15.8 0.5 fusion.17
  16.4 0.1 pad_maximum_fusion.refs_5_
  16.5 0.1 pad_maximum_fusion.1.refs_6_
  16.6 1.8 %collective-permute-start.11 = (bf16[512,256]{1,0:T(8,128)(2,1)}, bf16[512,256]{1,0:T(8,128)(2,1)S(1)}, u32[]{:S(2)}, u32[]{:S(2)}) collective-permute-start(bf16[512,256]{1,0:T(8,128)(2,1)} %refs_10_.1), channel_id=1, source_target_pairs={{0,4},{1,5},{2,6},{3,7},{4,0},{5,1},{6,2},{7,3},{8,12},{9,13},{10,... | collective-permute-start | bytes 786440 | tf_op jit(solution)/shard_map/ppermute | solution.py:514
  18.4 2.9 %collective-permute-done.4.refs_6_ = bf16[512,256]{1,0:T(8,128)(2,1)S(1)} collective-permute-done((bf16[512,256]{1,0:T(8,128)(2,1)}, bf16[512,256]{1,0:T(8,128)(2,1)S(1)}, u32[]{:S(2)}, u32[]{:S(2)}) %collective-permute-start.4) | collective-permute-done | bytes 262176 | tf_op jit(solution)/shard_map/ppermute | solution.py:514
  21.3 0.5 collective-permute-start.15
  21.9 1.3 %collective-permute-start.6 = (bf16[512,256]{1,0:T(8,128)(2,1)S(1)}, bf16[512,256]{1,0:T(8,128)(2,1)S(1)}, u32[]{:S(2)}, u32[]{:S(2)}) collective-permute-start(bf16[512,256]{1,0:T(8,128)(2,1)S(1)} %collective-permute-done.4.refs_6_), channel_id=1, source_target_pairs={{0,8},{1,9},{2,10},{3,11},{4,12},{5,13},{6,14},{7,15},{8,16},{9,17... | collective-permute-start | bytes 786440 | tf_op jit(solution)/shard_map/ppermute | solution.py:514
  23.1 1.0 %copy-done.5 = bf16[64,4096]{1,0:T(8,128)(2,1)S(1)} copy-done((bf16[64,4096]{1,0:T(8,128)(2,1)S(1)}, bf16[64,4096]{1,0:T(8,128)(2,1)}, u32[]{:S(2)}) %copy-start.5) | copy-done | bytes 524312
  24.2 0.7 copy-done.20
  24.9 6.1 %project.1 = (bf16[4,8,64,128]{3,2,1,0:T(8,128)(2,1)S(1)}, bf16[256,256]{1,0:T(8,128)(2,1)S(1)}, bf16[256,256]{1,0:T(8,128)(2,1)S(1)}) custom-call(bf16[64,4096]{1,0:T(8,128)(2,1)S(1)} %copy-done.5, bf16[64,4096]{1,0:T(8,128)(2,1)S(1)} %collective-permute-done.refs_1_, bf16[64,4096]{1,0:T(8,128)(2,1)S(1)} %collective-permute-done.1.refs_2_, ...), custom_call_target="tpu_custom_call" | custom-call | flops 7699999744 | tf_op jit(solution)/shard_map/project/pallas_call | solution.py:27
  30.9 1.4 %collective-permute-done.5.refs_5_ = bf16[512,256]{1,0:T(8,128)(2,1)S(1)} collective-permute-done((bf16[512,256]{1,0:T(8,128)(2,1)S(1)}, bf16[512,256]{1,0:T(8,128)(2,1)S(1)}, u32[]{:S(2)}, u32[]{:S(2)}) %collective-permute-start.5) | collective-permute-done | bytes 262176 | tf_op jit(solution)/shard_map/ppermute | solution.py:514
  32.4 0.5 collective-permute-start.16
  32.9 3.6 %collective-permute-done.6.refs_8_ = bf16[512,256]{1,0:T(8,128)(2,1)S(1)} collective-permute-done((bf16[512,256]{1,0:T(8,128)(2,1)S(1)}, bf16[512,256]{1,0:T(8,128)(2,1)S(1)}, u32[]{:S(2)}, u32[]{:S(2)}) %collective-permute-start.6) | collective-permute-done | bytes 262176 | tf_op jit(solution)/shard_map/ppermute | solution.py:514
  36.5 0.5 collective-permute-start.7
  37.0 0.0 collective-permute-done.10.refs_9_
  37.0 0.0 collective-permute-start.8
  37.0 0.0 collective-permute-done.11.refs_11_
  37.0 1.6 %collective-permute-start.13 = (bf16[512,256]{1,0:T(8,128)(2,1)S(1)}, bf16[512,256]{1,0:T(8,128)(2,1)S(1)}, u32[]{:S(2)}, u32[]{:S(2)}) collective-permute-start(bf16[512,256]{1,0:T(8,128)(2,1)S(1)} %collective-permute-done.6.refs_8_), channel_id=1, source_target_pairs={{0,4},{1,5},{2,6},{3,7},{4,0},{5,1},{6,2},{7,3},{8,12},{9,13},{10,... | collective-permute-start | bytes 786440 | tf_op jit(solution)/shard_map/ppermute | solution.py:514
  38.6 0.0 collective-permute-start.9
  38.6 9.5 %attend_first.1 = (f32[4,2,256,128]{3,2,1,0:T(8,128)S(1)}, f32[4,2,256,128]{3,2,1,0:T(8,128)S(1)}, f32[4,2,256,128]{3,2,1,0:T(8,128)S(1)}) custom-call(s32[3,4]{1,0:T(4,128)S(1)} %select_reduce_fusion.1.refs_0_, s32[8]{0:T(128)S(1)} %fusion.20.refs_1_, bf16[4,8,64,128]{3,2,1,0:T(8,128)(2,1)S(1)} %get-tuple-element.27.refs_2_, ...), custom_call_target="tpu_custom_call" | custom-call | flops 6600000000 | tf_op jit(solution)/shard_map/attend_first/pallas_call | solution.py:27
  48.1 0.0 collective-permute-done.16.refs_7_
  48.1 2.6 %attend_middle.2 = (f32[4,2,256,128]{3,2,1,0:T(8,128)S(1)}, f32[4,2,256,128]{3,2,1,0:T(8,128)S(1)}, f32[4,2,256,128]{3,2,1,0:T(8,128)S(1)}) custom-call(s32[3,4]{1,0:T(4,128)S(1)} %select_reduce_fusion.1.refs_0_, s32[8]{0:T(128)S(1)} %fusion.20.refs_1_, bf16[4,8,64,128]{3,2,1,0:T(8,128)(2,1)S(1)} %get-tuple-element.27.refs_2_, ...), custom_call_target="tpu_custom_call" | custom-call | flops 330000000 | tf_op jit(solution)/shard_map/attend_middle/pallas_call | solution.py:27
  50.8 0.1 collective-permute-done.9.refs_6_.refs_7_
  50.9 1.5 %collective-permute-start.12 = (bf16[512,256]{1,0:T(8,128)(2,1)S(1)}, bf16[512,256]{1,0:T(8,128)(2,1)S(1)}, u32[]{:S(2)}, u32[]{:S(2)}) collective-permute-start(bf16[512,256]{1,0:T(8,128)(2,1)S(1)} %collective-permute-done.8.refs_4_), channel_id=1, source_target_pairs={{0,4},{1,5},{2,6},{3,7},{4,0},{5,1},{6,2},{7,3},{8,12},{9,13},{10,... | collective-permute-start | bytes 786440 | tf_op jit(solution)/shard_map/ppermute | solution.py:514
  52.4 0.0 collective-permute-done.13.refs_5_.refs_6_
  52.4 1.0 %collective-permute-start.14 = (bf16[512,256]{1,0:T(8,128)(2,1)S(1)}, bf16[512,256]{1,0:T(8,128)(2,1)S(1)}, u32[]{:S(2)}, u32[]{:S(2)}) collective-permute-start(bf16[512,256]{1,0:T(8,128)(2,1)S(1)} %collective-permute-done.13.refs_5_.refs_6_), channel_id=1, source_target_pairs={{0,8},{1,9},{2,10},{3,11},{4,12},{5,13},{6,14},{7,15},{8,16},{9,17... | collective-permute-start | bytes 786440 | tf_op jit(solution)/shard_map/ppermute | solution.py:514
  53.4 3.0 %attend_middle.3 = (f32[2,2,256,128]{3,2,1,0:T(8,128)S(1)}, f32[2,2,256,128]{3,2,1,0:T(8,128)S(1)}, f32[2,2,256,128]{3,2,1,0:T(8,128)S(1)}) custom-call(s32[3,4]{1,0:T(4,128)S(1)} %select_reduce_fusion.1.refs_0_, s32[8]{0:T(128)S(1)} %fusion.20.refs_1_, bf16[4,8,64,128]{3,2,1,0:T(8,128)(2,1)S(1)} %get-tuple-element.27.refs_2_, ...), custom_call_target="tpu_custom_call" | custom-call | flops 4400000000 | tf_op jit(solution)/shard_map/attend_middle/pallas_call | solution.py:27
  56.5 0.8 collective-permute-done.12.refs_3_.refs_5_
  57.3 6.3 %collective-permute-done.14.refs_4_.refs_8_ = bf16[512,256]{1,0:T(8,128)(2,1)S(1)} collective-permute-done((bf16[512,256]{1,0:T(8,128)(2,1)S(1)}, bf16[512,256]{1,0:T(8,128)(2,1)S(1)}, u32[]{:S(2)}, u32[]{:S(2)}) %collective-permute-start.14) | collective-permute-done | bytes 262176 | tf_op jit(solution)/shard_map/ppermute | solution.py:514
  63.7 4.6 %attend_last.2 = (bf16[64,4096]{1,0:T(8,128)(2,1)S(1)}, bf16[64,4096]{1,0:T(8,128)(2,1)S(1)}) custom-call(s32[3,4]{1,0:T(4,128)S(1)} %select_reduce_fusion.1.refs_0_, s32[8]{0:T(128)S(1)} %fusion.20.refs_1_, bf16[4,8,64,128]{3,2,1,0:T(8,128)(2,1)S(1)} %get-tuple-element.27.refs_2_, bf16[512,256]{1,0:T(8,128)(2,1)S(1)} %collective-permute-done.12.refs_3_.refs_5_, ...), custom_call_target="tpu_custom_call" | custom-call | flops 4729999872 | tf_op jit(solution)/shard_map/attend_last/pallas_call | solution.py:27
  68.3 0.0 copy-start.9
  68.3 0.1 collective-permute-start.17
  68.4 0.1 broadcast_add_fusion
  68.5 0.1 reshape.130
  68.6 1.7 %collective-permute-done.17.refs_1_ = bf16[64,4096]{1,0:T(8,128)(2,1)S(1)} collective-permute-done((bf16[64,4096]{1,0:T(8,128)(2,1)S(1)}, bf16[64,4096]{1,0:T(8,128)(2,1)S(1)}, u32[]{:S(2)}, u32[]{:S(2)}) %collective-permute-start.17) | collective-permute-done | bytes 524320 | tf_op jit(solution)/shard_map/ppermute | solution.py:514
  70.3 0.1 add_up.3.refs_13_
  70.4 0.8 collective-permute-start.18
  71.3 8.1 %attend_last.3 = (bf16[64,4096]{1,0:T(8,128)(2,1)S(1)}, bf16[64,4096]{1,0:T(8,128)(2,1)S(1)}) custom-call(s32[3,4]{1,0:T(4,128)S(1)} %select_reduce_fusion.1.refs_0_, s32[8]{0:T(128)S(1)} %fusion.20.refs_1_, bf16[4,8,64,128]{3,2,1,0:T(8,128)(2,1)S(1)} %get-tuple-element.27.refs_2_, bf16[512,256]{1,0:T(8,128)(2,1)S(1)} %copy-done.9, ...), custom_call_target="tpu_custom_call" | custom-call | flops 6489999872 | tf_op jit(solution)/shard_map/attend_last/pallas_call | solution.py:27
  79.3 0.0 copy-start.21
  79.3 0.8 copy-done.21
  80.1 0.6 gather_fusion
  80.8 0.6 gather_fusion.1
  81.4 0.7 select_bitcast_fusion
  82.1 2.4 %collective-permute-done.18.refs_1_ = bf16[64,4096]{1,0:T(8,128)(2,1)S(1)} collective-permute-done((bf16[64,4096]{1,0:T(8,128)(2,1)S(1)}, bf16[64,4096]{1,0:T(8,128)(2,1)S(1)}, u32[]{:S(2)}, u32[]{:S(2)}) %collective-permute-start.18) | collective-permute-done | bytes 524320 | tf_op jit(solution)/shard_map/ppermute | solution.py:514
  84.5 1.0 %copy-done.22 = bf16[64,4096]{1,0:T(8,128)(2,1)S(1)} copy-done((bf16[64,4096]{1,0:T(8,128)(2,1)S(1)}, bf16[64,4096]{1,0:T(8,128)(2,1)}, u32[]{:S(2)}) %copy-start.22) | copy-done | bytes 524312
  85.5 0.1 add_up.4.refs_0_
  85.6 0.9 %add_up.5 = bf16[64,4096]{1,0:T(8,128)(2,1)} custom-call(f32[64,4096]{1,0:T(8,128)S(1)} %add_up.4.refs_0_, bf16[64,4096]{1,0:T(8,128)(2,1)S(1)} %collective-permute-done.19.refs_1_), custom_call_target="tpu_custom_call" | custom-call | flops 1100000000 | tf_op jit(solution)/shard_map/add_up/pallas_call | solution.py:27
  (62 shorter events, 0.2 us)
Async XLA Ops:
  0.6 15.2 %collective-permute-start.1 = (bf16[64,4096]{1,0:T(8,128)(2,1)}, bf16[64,4096]{1,0:T(8,128)(2,1)S(1)}, u32[]{:S(2)}, u32[]{:S(2)}) collective-permute-start(bf16[64,4096]{1,0:T(8,128)(2,1)} %refs_0_.1), channel_id=1, source_target_pairs={{0,2},{1,3},{2,0},{3,1},{4,6},{5,7},{6,4},{7,5},{8,10},{9,11},{10,... | collective-permute-start | bytes 1572872 | tf_op jit(solution)/shard_map/ppermute | solution.py:514
  3.7 17.7 %collective-permute-start = (bf16[64,4096]{1,0:T(8,128)(2,1)}, bf16[64,4096]{1,0:T(8,128)(2,1)S(1)}, u32[]{:S(2)}, u32[]{:S(2)}) collective-permute-start(bf16[64,4096]{1,0:T(8,128)(2,1)} %refs_0_.1), channel_id=1, source_target_pairs={{0,1},{1,0},{2,3},{3,2},{4,5},{5,4},{6,7},{7,6},{8,9},{9,8},{10,11... | collective-permute-start | bytes 1572872 | tf_op jit(solution)/shard_map/ppermute | solution.py:514
  3.7 33.3 %collective-permute-start.10 = (bf16[512,256]{1,0:T(8,128)(2,1)}, bf16[512,256]{1,0:T(8,128)(2,1)S(1)}, u32[]{:S(2)}, u32[]{:S(2)}) collective-permute-start(bf16[512,256]{1,0:T(8,128)(2,1)} %refs_8_.4), channel_id=1, source_target_pairs={{0,4},{1,5},{2,6},{3,7},{4,0},{5,1},{6,2},{7,3},{8,12},{9,13},{10,... | collective-permute-start | bytes 786440 | tf_op jit(solution)/shard_map/ppermute | solution.py:514
  5.2 11.4 %collective-permute-start.3 = (bf16[512,256]{1,0:T(8,128)(2,1)}, bf16[512,256]{1,0:T(8,128)(2,1)S(1)}, u32[]{:S(2)}, u32[]{:S(2)}) collective-permute-start(bf16[512,256]{1,0:T(8,128)(2,1)} %refs_8_.4), channel_id=1, source_target_pairs={{0,8},{1,9},{2,10},{3,11},{4,12},{5,13},{6,14},{7,15},{8,16},{9,17... | collective-permute-start | bytes 786440 | tf_op jit(solution)/shard_map/ppermute | solution.py:514
  6.7 14.6 %collective-permute-start.4 = (bf16[512,256]{1,0:T(8,128)(2,1)}, bf16[512,256]{1,0:T(8,128)(2,1)S(1)}, u32[]{:S(2)}, u32[]{:S(2)}) collective-permute-start(bf16[512,256]{1,0:T(8,128)(2,1)} %refs_10_.1), channel_id=1, source_target_pairs={{0,8},{1,9},{2,10},{3,11},{4,12},{5,13},{6,14},{7,15},{8,16},{9,17... | collective-permute-start | bytes 786440 | tf_op jit(solution)/shard_map/ppermute | solution.py:514
  15.8 6.1 %collective-permute-start.2 = (bf16[64,4096]{1,0:T(8,128)(2,1)S(1)}, bf16[64,4096]{1,0:T(8,128)(2,1)S(1)}, u32[]{:S(2)}, u32[]{:S(2)}) collective-permute-start(bf16[64,4096]{1,0:T(8,128)(2,1)S(1)} %collective-permute-done.1.refs_2_), channel_id=1, source_target_pairs={{0,1},{1,0},{2,3},{3,2},{4,5},{5,4},{6,7},{7,6},{8,9},{9,8},{10,11... | collective-permute-start | bytes 1572872 | tf_op jit(solution)/shard_map/ppermute | solution.py:514
  16.6 20.4 %collective-permute-start.11 = (bf16[512,256]{1,0:T(8,128)(2,1)}, bf16[512,256]{1,0:T(8,128)(2,1)S(1)}, u32[]{:S(2)}, u32[]{:S(2)}) collective-permute-start(bf16[512,256]{1,0:T(8,128)(2,1)} %refs_10_.1), channel_id=1, source_target_pairs={{0,4},{1,5},{2,6},{3,7},{4,0},{5,1},{6,2},{7,3},{8,12},{9,13},{10,... | collective-permute-start | bytes 786440 | tf_op jit(solution)/shard_map/ppermute | solution.py:514
  21.3 11.0 %collective-permute-start.5 = (bf16[512,256]{1,0:T(8,128)(2,1)S(1)}, bf16[512,256]{1,0:T(8,128)(2,1)S(1)}, u32[]{:S(2)}, u32[]{:S(2)}) collective-permute-start(bf16[512,256]{1,0:T(8,128)(2,1)S(1)} %collective-permute-done.3.refs_3_), channel_id=1, source_target_pairs={{0,8},{1,9},{2,10},{3,11},{4,12},{5,13},{6,14},{7,15},{8,16},{9,17... | collective-permute-start | bytes 786440 | tf_op jit(solution)/shard_map/ppermute | solution.py:514
  21.3 17.2 %collective-permute-start.15 = (bf16[512,256]{1,0:T(8,128)(2,1)S(1)}, bf16[512,256]{1,0:T(8,128)(2,1)S(1)}, u32[]{:S(2)}, u32[]{:S(2)}) collective-permute-start(bf16[512,256]{1,0:T(8,128)(2,1)S(1)} %collective-permute-done.3.refs_3_), channel_id=1, source_target_pairs={{0,4},{1,5},{2,6},{3,7},{4,0},{5,1},{6,2},{7,3},{8,12},{9,13},{10,... | collective-permute-start | bytes 786440 | tf_op jit(solution)/shard_map/ppermute | solution.py:514
  21.9 14.6 %collective-permute-start.6 = (bf16[512,256]{1,0:T(8,128)(2,1)S(1)}, bf16[512,256]{1,0:T(8,128)(2,1)S(1)}, u32[]{:S(2)}, u32[]{:S(2)}) collective-permute-start(bf16[512,256]{1,0:T(8,128)(2,1)S(1)} %collective-permute-done.4.refs_6_), channel_id=1, source_target_pairs={{0,8},{1,9},{2,10},{3,11},{4,12},{5,13},{6,14},{7,15},{8,16},{9,17... | collective-permute-start | bytes 786440 | tf_op jit(solution)/shard_map/ppermute | solution.py:514
  23.1 1.0 %copy-start.5 = (bf16[64,4096]{1,0:T(8,128)(2,1)S(1)}, bf16[64,4096]{1,0:T(8,128)(2,1)}, u32[]{:S(2)}) copy-start(bf16[64,4096]{1,0:T(8,128)(2,1)} %refs_0_.1) | copy-start | bytes 1572868
  24.2 0.7 copy-start.20
  24.9 13.7 %copy-start = (bf16[4608,256]{1,0:T(8,128)(2,1)S(1)}, bf16[4608,256]{1,0:T(8,128)(2,1)}, u32[]{:S(2)}) copy-start(bf16[4608,256]{1,0:T(8,128)(2,1)} %refs_6_.1) | copy-start | bytes 7077892
  24.9 13.7 %copy-start.1 = (bf16[4608,256]{1,0:T(8,128)(2,1)S(1)}, bf16[4608,256]{1,0:T(8,128)(2,1)}, u32[]{:S(2)}) copy-start(bf16[4608,256]{1,0:T(8,128)(2,1)} %refs_7_.3) | copy-start | bytes 7077892
  24.9 13.7 %copy-start.6 = (bf16[512,256]{1,0:T(8,128)(2,1)S(1)}, bf16[512,256]{1,0:T(8,128)(2,1)}, u32[]{:S(2)}) copy-start(bf16[512,256]{1,0:T(8,128)(2,1)} %refs_8_.4) | copy-start | bytes 786436
  24.9 13.7 %copy-start.7 = (bf16[512,256]{1,0:T(8,128)(2,1)S(1)}, bf16[512,256]{1,0:T(8,128)(2,1)}, u32[]{:S(2)}) copy-start(bf16[512,256]{1,0:T(8,128)(2,1)} %refs_10_.1) | copy-start | bytes 786436
  32.4 15.8 %collective-permute-start.16 = (bf16[512,256]{1,0:T(8,128)(2,1)S(1)}, bf16[512,256]{1,0:T(8,128)(2,1)S(1)}, u32[]{:S(2)}, u32[]{:S(2)}) collective-permute-start(bf16[512,256]{1,0:T(8,128)(2,1)S(1)} %collective-permute-done.4.refs_6_), channel_id=1, source_target_pairs={{0,4},{1,5},{2,6},{3,7},{4,0},{5,1},{6,2},{7,3},{8,12},{9,13},{10,... | collective-permute-start | bytes 786440 | tf_op jit(solution)/shard_map/ppermute | solution.py:514
  36.5 17.0 %collective-permute-start.7 = (bf16[512,256]{1,0:T(8,128)(2,1)S(1)}, bf16[512,256]{1,0:T(8,128)(2,1)S(1)}, u32[]{:S(2)}, u32[]{:S(2)}) collective-permute-start(bf16[512,256]{1,0:T(8,128)(2,1)S(1)} %collective-permute-done.5.refs_5_), channel_id=1, source_target_pairs={{0,4},{1,5},{2,6},{3,7},{4,0},{5,1},{6,2},{7,3},{8,12},{9,13},{10,... | collective-permute-start | bytes 786440 | tf_op jit(solution)/shard_map/ppermute | solution.py:514
  37.0 13.8 %collective-permute-start.8 = (bf16[512,256]{1,0:T(8,128)(2,1)S(1)}, bf16[512,256]{1,0:T(8,128)(2,1)S(1)}, u32[]{:S(2)}, u32[]{:S(2)}) collective-permute-start(bf16[512,256]{1,0:T(8,128)(2,1)S(1)} %collective-permute-done.5.refs_5_), channel_id=1, source_target_pairs={{0,8},{1,9},{2,10},{3,11},{4,12},{5,13},{6,14},{7,15},{8,16},{9,17... | collective-permute-start | bytes 786440 | tf_op jit(solution)/shard_map/ppermute | solution.py:514
  37.0 15.4 %collective-permute-start.13 = (bf16[512,256]{1,0:T(8,128)(2,1)S(1)}, bf16[512,256]{1,0:T(8,128)(2,1)S(1)}, u32[]{:S(2)}, u32[]{:S(2)}) collective-permute-start(bf16[512,256]{1,0:T(8,128)(2,1)S(1)} %collective-permute-done.6.refs_8_), channel_id=1, source_target_pairs={{0,4},{1,5},{2,6},{3,7},{4,0},{5,1},{6,2},{7,3},{8,12},{9,13},{10,... | collective-permute-start | bytes 786440 | tf_op jit(solution)/shard_map/ppermute | solution.py:514
  38.6 12.4 %collective-permute-start.9 = (bf16[512,256]{1,0:T(8,128)(2,1)S(1)}, bf16[512,256]{1,0:T(8,128)(2,1)S(1)}, u32[]{:S(2)}, u32[]{:S(2)}) collective-permute-start(bf16[512,256]{1,0:T(8,128)(2,1)S(1)} %collective-permute-done.6.refs_8_), channel_id=1, source_target_pairs={{0,8},{1,9},{2,10},{3,11},{4,12},{5,13},{6,14},{7,15},{8,16},{9,17... | collective-permute-start | bytes 786440 | tf_op jit(solution)/shard_map/ppermute | solution.py:514
  50.8 5.7 %copy-start.2 = (f32[4,2,256,128]{3,2,1,0:T(8,128)}, f32[4,2,256,128]{3,2,1,0:T(8,128)S(1)}, u32[]{:S(2)}) copy-start(f32[4,2,256,128]{3,2,1,0:T(8,128)S(1)} %get-tuple-element.40.refs_7_.refs_9_) | copy-start | bytes 3145732
  50.8 5.7 %copy-start.3 = (f32[4,2,256,128]{3,2,1,0:T(8,128)}, f32[4,2,256,128]{3,2,1,0:T(8,128)S(1)}, u32[]{:S(2)}) copy-start(f32[4,2,256,128]{3,2,1,0:T(8,128)S(1)} %get-tuple-element.41.refs_8_.refs_10_) | copy-start | bytes 3145732
  50.8 5.7 %copy-start.4 = (f32[4,2,256,128]{3,2,1,0:T(8,128)}, f32[4,2,256,128]{3,2,1,0:T(8,128)S(1)}, u32[]{:S(2)}) copy-start(f32[4,2,256,128]{3,2,1,0:T(8,128)S(1)} %get-tuple-element.42.refs_9_.refs_11_) | copy-start | bytes 3145732
  50.8 5.7 %copy-start.10 = (bf16[512,256]{1,0:T(8,128)(2,1)}, bf16[512,256]{1,0:T(8,128)(2,1)S(1)}, u32[]{:S(2)}) copy-start(bf16[512,256]{1,0:T(8,128)(2,1)S(1)} %collective-permute-done.8.refs_4_) | copy-start | bytes 786436
  50.9 5.5 %copy-start.14 = (bf16[512,256]{1,0:T(8,128)(2,1)}, bf16[512,256]{1,0:T(8,128)(2,1)S(1)}, u32[]{:S(2)}) copy-start(bf16[512,256]{1,0:T(8,128)(2,1)S(1)} %collective-permute-done.9.refs_6_.refs_7_) | copy-start | bytes 786436
  50.9 6.4 %collective-permute-start.12 = (bf16[512,256]{1,0:T(8,128)(2,1)S(1)}, bf16[512,256]{1,0:T(8,128)(2,1)S(1)}, u32[]{:S(2)}, u32[]{:S(2)}) collective-permute-start(bf16[512,256]{1,0:T(8,128)(2,1)S(1)} %collective-permute-done.8.refs_4_), channel_id=1, source_target_pairs={{0,4},{1,5},{2,6},{3,7},{4,0},{5,1},{6,2},{7,3},{8,12},{9,13},{10,... | collective-permute-start | bytes 786440 | tf_op jit(solution)/shard_map/ppermute | solution.py:514
  52.4 4.1 %copy-start.12 = (bf16[512,256]{1,0:T(8,128)(2,1)}, bf16[512,256]{1,0:T(8,128)(2,1)S(1)}, u32[]{:S(2)}) copy-start(bf16[512,256]{1,0:T(8,128)(2,1)S(1)} %collective-permute-done.13.refs_5_.refs_6_) | copy-start | bytes 786436
  52.4 11.2 %collective-permute-start.14 = (bf16[512,256]{1,0:T(8,128)(2,1)S(1)}, bf16[512,256]{1,0:T(8,128)(2,1)S(1)}, u32[]{:S(2)}, u32[]{:S(2)}) collective-permute-start(bf16[512,256]{1,0:T(8,128)(2,1)S(1)} %collective-permute-done.13.refs_5_.refs_6_), channel_id=1, source_target_pairs={{0,8},{1,9},{2,10},{3,11},{4,12},{5,13},{6,14},{7,15},{8,16},{9,17... | collective-permute-start | bytes 786440 | tf_op jit(solution)/shard_map/ppermute | solution.py:514
  53.4 3.1 %copy-start.8 = (bf16[512,256]{1,0:T(8,128)(2,1)}, bf16[512,256]{1,0:T(8,128)(2,1)S(1)}, u32[]{:S(2)}) copy-start(bf16[512,256]{1,0:T(8,128)(2,1)S(1)} %collective-permute-done.7.refs_3_) | copy-start | bytes 786436
  57.3 11.0 %copy-start.16 = (bf16[512,256]{1,0:T(8,128)(2,1)}, bf16[512,256]{1,0:T(8,128)(2,1)S(1)}, u32[]{:S(2)}) copy-start(bf16[512,256]{1,0:T(8,128)(2,1)S(1)} %collective-permute-done.12.refs_3_.refs_5_) | copy-start | bytes 786436
  63.7 4.6 %copy-start.18 = (bf16[512,256]{1,0:T(8,128)(2,1)}, bf16[512,256]{1,0:T(8,128)(2,1)S(1)}, u32[]{:S(2)}) copy-start(bf16[512,256]{1,0:T(8,128)(2,1)S(1)} %collective-permute-done.14.refs_4_.refs_8_) | copy-start | bytes 786436
  63.7 4.8 %copy-start.23 = (s32[4,8]{1,0:T(4,128)S(1)}, s32[4,8]{1,0:T(4,128)}, u32[]{:S(2)}) copy-start(s32[4,8]{1,0:T(4,128)} %param.29) | copy-start | bytes 388
  68.3 2.9 %copy-start.9 = (bf16[512,256]{1,0:T(8,128)(2,1)S(1)}, bf16[512,256]{1,0:T(8,128)(2,1)}, u32[]{:S(2)}) copy-start(bf16[512,256]{1,0:T(8,128)(2,1)} %copy-done.8) | copy-start | bytes 786436
  68.3 2.9 %copy-start.11 = (bf16[512,256]{1,0:T(8,128)(2,1)S(1)}, bf16[512,256]{1,0:T(8,128)(2,1)}, u32[]{:S(2)}) copy-start(bf16[512,256]{1,0:T(8,128)(2,1)} %copy-done.10) | copy-start | bytes 786436
  68.3 2.9 %copy-start.13 = (bf16[512,256]{1,0:T(8,128)(2,1)S(1)}, bf16[512,256]{1,0:T(8,128)(2,1)}, u32[]{:S(2)}) copy-start(bf16[512,256]{1,0:T(8,128)(2,1)} %copy-done.12) | copy-start | bytes 786436
  68.3 2.9 %copy-start.15 = (bf16[512,256]{1,0:T(8,128)(2,1)S(1)}, bf16[512,256]{1,0:T(8,128)(2,1)}, u32[]{:S(2)}) copy-start(bf16[512,256]{1,0:T(8,128)(2,1)} %copy-done.14) | copy-start | bytes 786436
  68.3 2.0 %collective-permute-start.17 = (bf16[64,4096]{1,0:T(8,128)(2,1)S(1)}, bf16[64,4096]{1,0:T(8,128)(2,1)S(1)}, u32[]{:S(2)}, u32[]{:S(2)}) collective-permute-start(bf16[64,4096]{1,0:T(8,128)(2,1)S(1)} %get-tuple-element.47), channel_id=1, source_target_pairs={{0,1},{1,0},{2,3},{3,2},{4,5},{5,4},{6,7},{7,6},{8,9},{9,8},{10,11... | collective-permute-start | bytes 1572872 | tf_op jit(solution)/shard_map/ppermute | solution.py:514
  68.6 2.7 %copy-start.17 = (bf16[512,256]{1,0:T(8,128)(2,1)S(1)}, bf16[512,256]{1,0:T(8,128)(2,1)}, u32[]{:S(2)}) copy-start(bf16[512,256]{1,0:T(8,128)(2,1)} %copy-done.16) | copy-start | bytes 786436
  68.6 2.7 %copy-start.19 = (bf16[512,256]{1,0:T(8,128)(2,1)S(1)}, bf16[512,256]{1,0:T(8,128)(2,1)}, u32[]{:S(2)}) copy-start(bf16[512,256]{1,0:T(8,128)(2,1)} %copy-done.18) | copy-start | bytes 786436
  70.4 14.0 %collective-permute-start.18 = (bf16[64,4096]{1,0:T(8,128)(2,1)S(1)}, bf16[64,4096]{1,0:T(8,128)(2,1)S(1)}, u32[]{:S(2)}, u32[]{:S(2)}) collective-permute-start(bf16[64,4096]{1,0:T(8,128)(2,1)S(1)} %add_up.3.refs_13_), channel_id=1, source_target_pairs={{0,2},{1,3},{2,0},{3,1},{4,6},{5,7},{6,4},{7,5},{8,10},{9,11},{10,... | collective-permute-start | bytes 1572872 | tf_op jit(solution)/shard_map/ppermute | solution.py:514
  79.3 0.8 copy-start.21
  80.1 5.5 %collective-permute-start.19 = (bf16[64,4096]{1,0:T(8,128)(2,1)S(1)}, bf16[64,4096]{1,0:T(8,128)(2,1)S(1)}, u32[]{:S(2)}, u32[]{:S(2)}) collective-permute-start(bf16[64,4096]{1,0:T(8,128)(2,1)S(1)} %get-tuple-element.49), channel_id=1, source_target_pairs={{0,1},{1,0},{2,3},{3,2},{4,5},{5,4},{6,7},{7,6},{8,9},{9,8},{10,11... | collective-permute-start | bytes 1572872 | tf_op jit(solution)/shard_map/ppermute | solution.py:514
  84.5 1.0 %copy-start.22 = (bf16[64,4096]{1,0:T(8,128)(2,1)S(1)}, bf16[64,4096]{1,0:T(8,128)(2,1)}, u32[]{:S(2)}) copy-start(bf16[64,4096]{1,0:T(8,128)(2,1)} %copy-done.21) | copy-start | bytes 1572868

commit v2 on v1

--- a/solution.py
+++ b/solution.py
@@ -336,7 +336,8 @@
     copies = fetch_all(sources, held, sems)
     reqs = outs[0].shape[0]
     for src, dst in zip(ins, outs):
-        dst[...] = src[offset : offset + reqs]
+        lead = 0 if src.shape[0] == reqs else offset
+        dst[...] = src[lead : lead + reqs]
     for copy in copies:
         copy.wait()
 
@@ -347,7 +348,7 @@
     lax.fori_loop(0, reqs, one_request, 0)
 
 
-def attend_middle(queries, info, bases, shards, span, state, offset, reqs, microseconds=0.3):
+def attend_middle(queries, info, bases, shards, span, state, offset, reqs, microseconds=2.7):
     shards = shards[span[0] : span[1]]
     _, n_heads, tree, _ = queries.shape
     kv_local = shards[0][0].shape[1] // HD
@@ -572,14 +573,14 @@
         pass_on(steps - 1, state[0])
         shards += [ring[-1], side[-1]]
         n = len(shards)
-        state = attend_middle(queries, info, bases, shards, (2, 5), state, 0, reqs)
-        far_state = attend_middle(queries, info, bases, shards, (5, n - 1), state, 2, 2, 4)
+        far_state = attend_middle(queries, info, bases, shards, (2, 5), state, 2, 2)
+        far_state = attend_middle(queries, info, bases, shards, (5, n - 1), far_state, 2, 2, 1.1)
         final = functools.partial(attend_last, queries, info, bases, shards, w_out=w_out, reqs=2)
         kept, away = final((n - 1, n), far_state, offset=2)
         got = send(away, core_pairs)
         summed = add_up(kept, got)
         far = send(summed, y_pairs)
-        kept, away = final((5, n), state, offset=0, after=(summed,))
+        kept, away = final((2, n), state, offset=0, after=(summed,))
         got = send(away, core_pairs)
         mixed_rows = add_up(add_up(kept, far, dtype=jnp.float32), got)
     else:

time: 87.1 us -> 86.6 us (level)
  waiting for transfers between devices: 22.1 us -> 17.8 us
  Pallas kernels: 34.9 us -> 37 us
  local copies, waits for them, and re-layouts: 5.83 us -> 7.8 us
    ppermute x20, waiting for transfers between devices: 22.1 us -> 17.8 us  [body(): send = lambda a, p: lax.ppermute(a, AXES, p)]
    pallas_call x9, Pallas kernels: 34.9 us -> 37 us  [call(): pl.pallas_call(wrapped, in_specs=in_specs + [HBM] * len(after), out_specs...]
    unnamed x48 -> x52, local copies, waits for them, and re-layouts: 3.67 us -> 5.64 us
  transfers between devices with their start and end apart: 20 -> 20, of which waited for: 9 -> 7; matrix products, arithmetic and copies ran while one was open for 9% -> 9% of each run, Pallas kernels for 34% -> 36%
where the time goes in v2:
time: 86.6 us; the launch traced here: 85.9 us
  Pallas kernels  37 us (43%)
  waiting for transfers between devices  17.8 us (21%)
  starting transfers between devices  16.9 us (20%)
  local copies, waits for them, and re-layouts  7.8 us (9%)
  other arithmetic  4.19 us (5%)
  matrix products  1.15 us (1%)
  between operations  1.01 us (1%)
    pallas_call x9, Pallas kernels, call(): pl.pallas_call(wrapped, in_specs=in_specs + [HBM] * len(after), out_specs...  37 us
    ppermute x20, waiting for transfers between devices, body(): send = lambda a, p: lax.ppermute(a, AXES, p)  17.8 us
    ppermute x20, starting transfers between devices, body(): send = lambda a, p: lax.ppermute(a, AXES, p)  16.9 us
    unnamed x52, local copies, waits for them, and re-layouts  5.64 us
  transfers between devices with their start and end apart: 20, of which 7 were waited for; matrix products, arithmetic and copies ran while one was open for 9% of the time, Pallas kernels for 36%

profile of v2, /device:TPU:0, one launch (start us, length us, event | category | flops | bytes accessed | tf_op | source)
XLA Modules:
  0.0 85.9 jit_solution(10513606342504287471)
XLA Ops:
  0.6 3.0 %collective-permute-start.1 = (bf16[64,4096]{1,0:T(8,128)(2,1)}, bf16[64,4096]{1,0:T(8,128)(2,1)S(1)}, u32[]{:S(2)}, u32[]{:S(2)}) collective-permute-start(bf16[64,4096]{1,0:T(8,128)(2,1)} %refs_0_.1), channel_id=1, source_target_pairs={{0,2},{1,3},{2,0},{3,1},{4,6},{5,7},{6,4},{7,5},{8,10},{9,11},{10,... | collective-permute-start | bytes 1572872 | tf_op jit(solution)/shard_map/ppermute | solution.py:515
  3.7 1.5 %collective-permute-start.11 = (bf16[512,256]{1,0:T(8,128)(2,1)}, bf16[512,256]{1,0:T(8,128)(2,1)S(1)}, u32[]{:S(2)}, u32[]{:S(2)}) collective-permute-start(bf16[512,256]{1,0:T(8,128)(2,1)} %refs_8_.4), channel_id=1, source_target_pairs={{0,4},{1,5},{2,6},{3,7},{4,0},{5,1},{6,2},{7,3},{8,12},{9,13},{10,... | collective-permute-start | bytes 786440 | tf_op jit(solution)/shard_map/ppermute | solution.py:515
  5.2 1.6 %collective-permute-start.3 = (bf16[512,256]{1,0:T(8,128)(2,1)}, bf16[512,256]{1,0:T(8,128)(2,1)S(1)}, u32[]{:S(2)}, u32[]{:S(2)}) collective-permute-start(bf16[512,256]{1,0:T(8,128)(2,1)} %refs_8_.4), channel_id=1, source_target_pairs={{0,8},{1,9},{2,10},{3,11},{4,12},{5,13},{6,14},{7,15},{8,16},{9,17... | collective-permute-start | bytes 786440 | tf_op jit(solution)/shard_map/ppermute | solution.py:515
  6.7 1.6 %collective-permute-start.4 = (bf16[512,256]{1,0:T(8,128)(2,1)}, bf16[512,256]{1,0:T(8,128)(2,1)S(1)}, u32[]{:S(2)}, u32[]{:S(2)}) collective-permute-start(bf16[512,256]{1,0:T(8,128)(2,1)} %refs_10_.1), channel_id=1, source_target_pairs={{0,8},{1,9},{2,10},{3,11},{4,12},{5,13},{6,14},{7,15},{8,16},{9,17... | collective-permute-start | bytes 786440 | tf_op jit(solution)/shard_map/ppermute | solution.py:515
  8.3 0.7 dynamic-slice_bitcast_fusion
  9.1 0.2 reduce-window.4
  9.2 0.7 fusion.24
  10.0 0.1 iota_compare_fusion.2
  10.0 0.7 pad_add_fusion
  10.7 0.1 select_reduce_fusion.1.refs_0_
  10.9 0.8 select_reduce_fusion
  11.6 0.5 fusion.1
  12.1 0.3 fusion.3
  12.4 0.4 fusion.28
  12.8 0.1 add_convert_fusion
  12.9 0.1 convert_element_type.52
  13.0 2.8 %collective-permute-done.1.refs_2_ = bf16[64,4096]{1,0:T(8,128)(2,1)S(1)} collective-permute-done((bf16[64,4096]{1,0:T(8,128)(2,1)}, bf16[64,4096]{1,0:T(8,128)(2,1)S(1)}, u32[]{:S(2)}, u32[]{:S(2)}) %collective-permute-start.1) | collective-permute-done | bytes 524320 | tf_op jit(solution)/shard_map/ppermute | solution.py:515
  15.8 0.5 fusion.17
  16.4 0.1 pad_maximum_fusion.refs_5_
  16.5 0.1 pad_maximum_fusion.1.refs_6_
  16.6 1.8 %collective-permute-start.12 = (bf16[512,256]{1,0:T(8,128)(2,1)}, bf16[512,256]{1,0:T(8,128)(2,1)S(1)}, u32[]{:S(2)}, u32[]{:S(2)}) collective-permute-start(bf16[512,256]{1,0:T(8,128)(2,1)} %refs_10_.1), channel_id=1, source_target_pairs={{0,4},{1,5},{2,6},{3,7},{4,0},{5,1},{6,2},{7,3},{8,12},{9,13},{10,... | collective-permute-start | bytes 786440 | tf_op jit(solution)/shard_map/ppermute | solution.py:515
  18.4 2.9 %collective-permute-done.4.refs_6_.refs_9_ = bf16[512,256]{1,0:T(8,128)(2,1)S(1)} collective-permute-done((bf16[512,256]{1,0:T(8,128)(2,1)}, bf16[512,256]{1,0:T(8,128)(2,1)S(1)}, u32[]{:S(2)}, u32[]{:S(2)}) %collective-permute-start.4) | collective-permute-done | bytes 262176 | tf_op jit(solution)/shard_map/ppermute | solution.py:515
  21.3 0.5 collective-permute-start.14
  21.9 1.3 %collective-permute-start.6 = (bf16[512,256]{1,0:T(8,128)(2,1)S(1)}, bf16[512,256]{1,0:T(8,128)(2,1)S(1)}, u32[]{:S(2)}, u32[]{:S(2)}) collective-permute-start(bf16[512,256]{1,0:T(8,128)(2,1)S(1)} %collective-permute-done.3.refs_3_), channel_id=1, source_target_pairs={{0,8},{1,9},{2,10},{3,11},{4,12},{5,13},{6,14},{7,15},{8,16},{9,17... | collective-permute-start | bytes 786440 | tf_op jit(solution)/shard_map/ppermute | solution.py:515
  23.1 1.0 %copy-done.2 = bf16[64,4096]{1,0:T(8,128)(2,1)S(1)} copy-done((bf16[64,4096]{1,0:T(8,128)(2,1)S(1)}, bf16[64,4096]{1,0:T(8,128)(2,1)}, u32[]{:S(2)}) %copy-start.2) | copy-done | bytes 524312
  24.2 0.7 copy-done.16
  24.9 6.1 %project.1 = (bf16[4,8,64,128]{3,2,1,0:T(8,128)(2,1)S(1)}, bf16[256,256]{1,0:T(8,128)(2,1)S(1)}, bf16[256,256]{1,0:T(8,128)(2,1)S(1)}) custom-call(bf16[64,4096]{1,0:T(8,128)(2,1)S(1)} %copy-done.2, bf16[64,4096]{1,0:T(8,128)(2,1)S(1)} %collective-permute-done.refs_1_, bf16[64,4096]{1,0:T(8,128)(2,1)S(1)} %collective-permute-done.1.refs_2_, ...), custom_call_target="tpu_custom_call" | custom-call | flops 7699999744 | tf_op jit(solution)/shard_map/project/pallas_call | solution.py:27
  30.9 0.0 copy-start.17
  31.0 5.5 %collective-permute-done.6.refs_5_ = bf16[512,256]{1,0:T(8,128)(2,1)S(1)} collective-permute-done((bf16[512,256]{1,0:T(8,128)(2,1)S(1)}, bf16[512,256]{1,0:T(8,128)(2,1)S(1)}, u32[]{:S(2)}, u32[]{:S(2)}) %collective-permute-start.6) | collective-permute-done | bytes 262176 | tf_op jit(solution)/shard_map/ppermute | solution.py:515
  36.5 0.5 collective-permute-start.5
  37.0 0.0 collective-permute-done.7.refs_8_.refs_11_
  37.0 0.0 collective-permute-start.10
  37.0 0.0 collective-permute-done.11.refs_9_
  37.0 1.6 %collective-permute-start.15 = (bf16[512,256]{1,0:T(8,128)(2,1)S(1)}, bf16[512,256]{1,0:T(8,128)(2,1)S(1)}, u32[]{:S(2)}, u32[]{:S(2)}) collective-permute-start(bf16[512,256]{1,0:T(8,128)(2,1)S(1)} %collective-permute-done.7.refs_8_.refs_11_), channel_id=1, source_target_pairs={{0,4},{1,5},{2,6},{3,7},{4,0},{5,1},{6,2},{7,3},{8,12},{9,13},{10,... | collective-permute-start | bytes 786440 | tf_op jit(solution)/shard_map/ppermute | solution.py:515
  38.6 9.6 %attend_first.1 = (f32[4,2,256,128]{3,2,1,0:T(8,128)S(1)}, f32[4,2,256,128]{3,2,1,0:T(8,128)S(1)}, f32[4,2,256,128]{3,2,1,0:T(8,128)S(1)}) custom-call(s32[3,4]{1,0:T(4,128)S(1)} %select_reduce_fusion.1.refs_0_, s32[8]{0:T(128)S(1)} %fusion.20.refs_1_, bf16[4,8,64,128]{3,2,1,0:T(8,128)(2,1)S(1)} %get-tuple-element.27.refs_2_, ...), custom_call_target="tpu_custom_call" | custom-call | flops 6600000000 | tf_op jit(solution)/shard_map/attend_first/pallas_call | solution.py:27
  48.2 1.3 %collective-permute-start.8 = (bf16[512,256]{1,0:T(8,128)(2,1)S(1)}, bf16[512,256]{1,0:T(8,128)(2,1)S(1)}, u32[]{:S(2)}, u32[]{:S(2)}) collective-permute-start(bf16[512,256]{1,0:T(8,128)(2,1)S(1)} %collective-permute-done.6.refs_5_), channel_id=1, source_target_pairs={{0,4},{1,5},{2,6},{3,7},{4,0},{5,1},{6,2},{7,3},{8,12},{9,13},{10,... | collective-permute-start | bytes 786440 | tf_op jit(solution)/shard_map/ppermute | solution.py:515
  49.5 1.4 %collective-permute-done.9.refs_4_.refs_7_ = bf16[512,256]{1,0:T(8,128)(2,1)S(1)} collective-permute-done((bf16[512,256]{1,0:T(8,128)(2,1)S(1)}, bf16[512,256]{1,0:T(8,128)(2,1)S(1)}, u32[]{:S(2)}, u32[]{:S(2)}) %collective-permute-start.9) | collective-permute-done | bytes 262176 | tf_op jit(solution)/shard_map/ppermute | solution.py:515
  50.9 1.5 %collective-permute-start.13 = (bf16[512,256]{1,0:T(8,128)(2,1)S(1)}, bf16[512,256]{1,0:T(8,128)(2,1)S(1)}, u32[]{:S(2)}, u32[]{:S(2)}) collective-permute-start(bf16[512,256]{1,0:T(8,128)(2,1)S(1)} %collective-permute-done.9.refs_4_.refs_7_), channel_id=1, source_target_pairs={{0,4},{1,5},{2,6},{3,7},{4,0},{5,1},{6,2},{7,3},{8,12},{9,13},{10,... | collective-permute-start | bytes 786440 | tf_op jit(solution)/shard_map/ppermute | solution.py:515
  52.4 0.0 collective-permute-done.15.refs_5_.refs_12_
  52.4 0.0 collective-permute-start.16
  52.4 0.0 collective-permute-done.14.refs_7_.refs_10_
  52.5 1.7 %attend_middle.2 = (f32[2,2,256,128]{3,2,1,0:T(8,128)S(1)}, f32[2,2,256,128]{3,2,1,0:T(8,128)S(1)}, f32[2,2,256,128]{3,2,1,0:T(8,128)S(1)}) custom-call(s32[3,4]{1,0:T(4,128)S(1)} %select_reduce_fusion.1.refs_0_, s32[8]{0:T(128)S(1)} %fusion.20.refs_1_, bf16[4,8,64,128]{3,2,1,0:T(8,128)(2,1)S(1)} %get-tuple-element.27.refs_2_, ...), custom_call_target="tpu_custom_call" | custom-call | flops 2969999872 | tf_op jit(solution)/shard_map/attend_middle/pallas_call | solution.py:27
  54.2 3.2 %collective-permute-done.8.refs_3_.refs_6_ = bf16[512,256]{1,0:T(8,128)(2,1)S(1)} collective-permute-done((bf16[512,256]{1,0:T(8,128)(2,1)S(1)}, bf16[512,256]{1,0:T(8,128)(2,1)S(1)}, u32[]{:S(2)}, u32[]{:S(2)}) %collective-permute-start.8) | collective-permute-done | bytes 262176 | tf_op jit(solution)/shard_map/ppermute | solution.py:515
  57.4 3.0 %attend_middle.3 = (f32[2,2,256,128]{3,2,1,0:T(8,128)S(1)}, f32[2,2,256,128]{3,2,1,0:T(8,128)S(1)}, f32[2,2,256,128]{3,2,1,0:T(8,128)S(1)}) custom-call(s32[3,4]{1,0:T(4,128)S(1)} %select_reduce_fusion.1.refs_0_, s32[8]{0:T(128)S(1)} %fusion.20.refs_1_, bf16[4,8,64,128]{3,2,1,0:T(8,128)(2,1)S(1)} %get-tuple-element.27.refs_2_, ...), custom_call_target="tpu_custom_call" | custom-call | flops 1210000000 | tf_op jit(solution)/shard_map/attend_middle/pallas_call | solution.py:27
  60.4 0.2 collective-permute-done.16.refs_4_.refs_14_
  60.6 4.6 %attend_last.2 = (bf16[64,4096]{1,0:T(8,128)(2,1)S(1)}, bf16[64,4096]{1,0:T(8,128)(2,1)S(1)}) custom-call(s32[3,4]{1,0:T(4,128)S(1)} %select_reduce_fusion.1.refs_0_, s32[8]{0:T(128)S(1)} %fusion.20.refs_1_, bf16[4,8,64,128]{3,2,1,0:T(8,128)(2,1)S(1)} %get-tuple-element.27.refs_2_, bf16[512,256]{1,0:T(8,128)(2,1)S(1)} %collective-permute-done.13.refs_3_.refs_8_, ...), custom_call_target="tpu_custom_call" | custom-call | flops 4729999872 | tf_op jit(solution)/shard_map/attend_last/pallas_call | solution.py:27
  65.3 0.8 copy-done.20
  66.1 0.1 broadcast_add_fusion
  66.1 0.1 reshape.130
  66.2 1.7 %collective-permute-done.17.refs_1_ = bf16[64,4096]{1,0:T(8,128)(2,1)S(1)} collective-permute-done((bf16[64,4096]{1,0:T(8,128)(2,1)S(1)}, bf16[64,4096]{1,0:T(8,128)(2,1)S(1)}, u32[]{:S(2)}, u32[]{:S(2)}) %collective-permute-start.17) | collective-permute-done | bytes 524320 | tf_op jit(solution)/shard_map/ppermute | solution.py:515
  68.0 1.0 %copy-done.21 = bf16[64,4096]{1,0:T(8,128)(2,1)S(1)} copy-done((bf16[64,4096]{1,0:T(8,128)(2,1)S(1)}, bf16[64,4096]{1,0:T(8,128)(2,1)}, u32[]{:S(2)}) %copy-start.21) | copy-done | bytes 524312
  69.0 0.1 add_up.3.refs_19_
  69.1 0.6 collective-permute-start.18
  69.8 0.1 copy-done.3
  69.9 10.9 %attend_last.3 = (bf16[64,4096]{1,0:T(8,128)(2,1)S(1)}, bf16[64,4096]{1,0:T(8,128)(2,1)}) custom-call(s32[3,4]{1,0:T(4,128)S(1)} %select_reduce_fusion.1.refs_0_, s32[8]{0:T(128)S(1)} %fusion.20.refs_1_, bf16[4,8,64,128]{3,2,1,0:T(8,128)(2,1)} %copy-done.17, bf16[512,256]{1,0:T(8,128)(2,1)S(1)} %collective-permute-done.3.refs_3_, ...), custom_call_target="tpu_custom_call" | custom-call | flops 9130000384 | tf_op jit(solution)/shard_map/attend_last/pallas_call | solution.py:27
  80.9 0.0 copy-start.18
  80.9 0.8 copy-done.18
  81.7 0.1 collective-permute-start.19
  81.8 0.6 gather_fusion
  82.4 0.6 gather_fusion.1
  83.0 0.7 select_bitcast_fusion
  83.7 1.0 %copy-done.19 = bf16[64,4096]{1,0:T(8,128)(2,1)S(1)} copy-done((bf16[64,4096]{1,0:T(8,128)(2,1)S(1)}, bf16[64,4096]{1,0:T(8,128)(2,1)}, u32[]{:S(2)}) %copy-start.19) | copy-done | bytes 524312
  84.8 0.1 add_up.4.refs_0_
  84.9 0.9 %add_up.5 = bf16[64,4096]{1,0:T(8,128)(2,1)} custom-call(f32[64,4096]{1,0:T(8,128)S(1)} %add_up.4.refs_0_, bf16[64,4096]{1,0:T(8,128)(2,1)S(1)} %collective-permute-done.19.refs_1_), custom_call_target="tpu_custom_call" | custom-call | flops 1100000000 | tf_op jit(solution)/shard_map/add_up/pallas_call | solution.py:27
  (66 shorter events, 0.2 us)
Async XLA Ops:
  0.6 15.2 %collective-permute-start.1 = (bf16[64,4096]{1,0:T(8,128)(2,1)}, bf16[64,4096]{1,0:T(8,128)(2,1)S(1)}, u32[]{:S(2)}, u32[]{:S(2)}) collective-permute-start(bf16[64,4096]{1,0:T(8,128)(2,1)} %refs_0_.1), channel_id=1, source_target_pairs={{0,2},{1,3},{2,0},{3,1},{4,6},{5,7},{6,4},{7,5},{8,10},{9,11},{10,... | collective-permute-start | bytes 1572872 | tf_op jit(solution)/shard_map/ppermute | solution.py:515
  3.7 17.7 %collective-permute-start = (bf16[64,4096]{1,0:T(8,128)(2,1)}, bf16[64,4096]{1,0:T(8,128)(2,1)S(1)}, u32[]{:S(2)}, u32[]{:S(2)}) collective-permute-start(bf16[64,4096]{1,0:T(8,128)(2,1)} %refs_0_.1), channel_id=1, source_target_pairs={{0,1},{1,0},{2,3},{3,2},{4,5},{5,4},{6,7},{7,6},{8,9},{9,8},{10,11... | collective-permute-start | bytes 1572872 | tf_op jit(solution)/shard_map/ppermute | solution.py:515
  3.7 33.3 %collective-permute-start.11 = (bf16[512,256]{1,0:T(8,128)(2,1)}, bf16[512,256]{1,0:T(8,128)(2,1)S(1)}, u32[]{:S(2)}, u32[]{:S(2)}) collective-permute-start(bf16[512,256]{1,0:T(8,128)(2,1)} %refs_8_.4), channel_id=1, source_target_pairs={{0,4},{1,5},{2,6},{3,7},{4,0},{5,1},{6,2},{7,3},{8,12},{9,13},{10,... | collective-permute-start | bytes 786440 | tf_op jit(solution)/shard_map/ppermute | solution.py:515
  5.2 11.4 %collective-permute-start.3 = (bf16[512,256]{1,0:T(8,128)(2,1)}, bf16[512,256]{1,0:T(8,128)(2,1)S(1)}, u32[]{:S(2)}, u32[]{:S(2)}) collective-permute-start(bf16[512,256]{1,0:T(8,128)(2,1)} %refs_8_.4), channel_id=1, source_target_pairs={{0,8},{1,9},{2,10},{3,11},{4,12},{5,13},{6,14},{7,15},{8,16},{9,17... | collective-permute-start | bytes 786440 | tf_op jit(solution)/shard_map/ppermute | solution.py:515
  6.7 14.6 %collective-permute-start.4 = (bf16[512,256]{1,0:T(8,128)(2,1)}, bf16[512,256]{1,0:T(8,128)(2,1)S(1)}, u32[]{:S(2)}, u32[]{:S(2)}) collective-permute-start(bf16[512,256]{1,0:T(8,128)(2,1)} %refs_10_.1), channel_id=1, source_target_pairs={{0,8},{1,9},{2,10},{3,11},{4,12},{5,13},{6,14},{7,15},{8,16},{9,17... | collective-permute-start | bytes 786440 | tf_op jit(solution)/shard_map/ppermute | solution.py:515
  15.8 6.1 %collective-permute-start.2 = (bf16[64,4096]{1,0:T(8,128)(2,1)S(1)}, bf16[64,4096]{1,0:T(8,128)(2,1)S(1)}, u32[]{:S(2)}, u32[]{:S(2)}) collective-permute-start(bf16[64,4096]{1,0:T(8,128)(2,1)S(1)} %collective-permute-done.1.refs_2_), channel_id=1, source_target_pairs={{0,1},{1,0},{2,3},{3,2},{4,5},{5,4},{6,7},{7,6},{8,9},{9,8},{10,11... | collective-permute-start | bytes 1572872 | tf_op jit(solution)/shard_map/ppermute | solution.py:515
  16.6 22.0 %collective-permute-start.12 = (bf16[512,256]{1,0:T(8,128)(2,1)}, bf16[512,256]{1,0:T(8,128)(2,1)S(1)}, u32[]{:S(2)}, u32[]{:S(2)}) collective-permute-start(bf16[512,256]{1,0:T(8,128)(2,1)} %refs_10_.1), channel_id=1, source_target_pairs={{0,4},{1,5},{2,6},{3,7},{4,0},{5,1},{6,2},{7,3},{8,12},{9,13},{10,... | collective-permute-start | bytes 786440 | tf_op jit(solution)/shard_map/ppermute | solution.py:515
  21.3 15.7 %collective-permute-start.7 = (bf16[512,256]{1,0:T(8,128)(2,1)S(1)}, bf16[512,256]{1,0:T(8,128)(2,1)S(1)}, u32[]{:S(2)}, u32[]{:S(2)}) collective-permute-start(bf16[512,256]{1,0:T(8,128)(2,1)S(1)} %collective-permute-done.4.refs_6_.refs_9_), channel_id=1, source_target_pairs={{0,8},{1,9},{2,10},{3,11},{4,12},{5,13},{6,14},{7,15},{8,16},{9,17... | collective-permute-start | bytes 786440 | tf_op jit(solution)/shard_map/ppermute | solution.py:515
  21.3 31.1 %collective-permute-start.14 = (bf16[512,256]{1,0:T(8,128)(2,1)S(1)}, bf16[512,256]{1,0:T(8,128)(2,1)S(1)}, u32[]{:S(2)}, u32[]{:S(2)}) collective-permute-start(bf16[512,256]{1,0:T(8,128)(2,1)S(1)} %collective-permute-done.4.refs_6_.refs_9_), channel_id=1, source_target_pairs={{0,4},{1,5},{2,6},{3,7},{4,0},{5,1},{6,2},{7,3},{8,12},{9,13},{10,... | collective-permute-start | bytes 786440 | tf_op jit(solution)/shard_map/ppermute | solution.py:515
  21.9 14.6 %collective-permute-start.6 = (bf16[512,256]{1,0:T(8,128)(2,1)S(1)}, bf16[512,256]{1,0:T(8,128)(2,1)S(1)}, u32[]{:S(2)}, u32[]{:S(2)}) collective-permute-start(bf16[512,256]{1,0:T(8,128)(2,1)S(1)} %collective-permute-done.3.refs_3_), channel_id=1, source_target_pairs={{0,8},{1,9},{2,10},{3,11},{4,12},{5,13},{6,14},{7,15},{8,16},{9,17... | collective-permute-start | bytes 786440 | tf_op jit(solution)/shard_map/ppermute | solution.py:515
  23.1 1.0 %copy-start.2 = (bf16[64,4096]{1,0:T(8,128)(2,1)S(1)}, bf16[64,4096]{1,0:T(8,128)(2,1)}, u32[]{:S(2)}) copy-start(bf16[64,4096]{1,0:T(8,128)(2,1)} %refs_0_.1) | copy-start | bytes 1572868
  24.2 0.7 copy-start.16
  24.9 13.7 %copy-start = (bf16[4608,256]{1,0:T(8,128)(2,1)S(1)}, bf16[4608,256]{1,0:T(8,128)(2,1)}, u32[]{:S(2)}) copy-start(bf16[4608,256]{1,0:T(8,128)(2,1)} %refs_6_.1) | copy-start | bytes 7077892
  24.9 13.7 %copy-start.1 = (bf16[4608,256]{1,0:T(8,128)(2,1)S(1)}, bf16[4608,256]{1,0:T(8,128)(2,1)}, u32[]{:S(2)}) copy-start(bf16[4608,256]{1,0:T(8,128)(2,1)} %refs_7_.3) | copy-start | bytes 7077892
  24.9 13.7 %copy-start.4 = (bf16[512,256]{1,0:T(8,128)(2,1)S(1)}, bf16[512,256]{1,0:T(8,128)(2,1)}, u32[]{:S(2)}) copy-start(bf16[512,256]{1,0:T(8,128)(2,1)} %refs_8_.4) | copy-start | bytes 786436
  24.9 13.7 %copy-start.5 = (bf16[512,256]{1,0:T(8,128)(2,1)S(1)}, bf16[512,256]{1,0:T(8,128)(2,1)}, u32[]{:S(2)}) copy-start(bf16[512,256]{1,0:T(8,128)(2,1)} %refs_10_.1) | copy-start | bytes 786436
  30.9 29.7 %copy-start.17 = (bf16[4,8,64,128]{3,2,1,0:T(8,128)(2,1)}, bf16[4,8,64,128]{3,2,1,0:T(8,128)(2,1)S(1)}, u32[]{:S(2)}) copy-start(bf16[4,8,64,128]{3,2,1,0:T(8,128)(2,1)S(1)} %get-tuple-element.27.refs_2_) | copy-start | bytes 1572868
  36.5 16.0 %collective-permute-start.5 = (bf16[512,256]{1,0:T(8,128)(2,1)S(1)}, bf16[512,256]{1,0:T(8,128)(2,1)S(1)}, u32[]{:S(2)}, u32[]{:S(2)}) collective-permute-start(bf16[512,256]{1,0:T(8,128)(2,1)S(1)} %collective-permute-done.3.refs_3_), channel_id=1, source_target_pairs={{0,4},{1,5},{2,6},{3,7},{4,0},{5,1},{6,2},{7,3},{8,12},{9,13},{10,... | collective-permute-start | bytes 786440 | tf_op jit(solution)/shard_map/ppermute | solution.py:515
  37.0 11.2 %collective-permute-start.10 = (bf16[512,256]{1,0:T(8,128)(2,1)S(1)}, bf16[512,256]{1,0:T(8,128)(2,1)S(1)}, u32[]{:S(2)}, u32[]{:S(2)}) collective-permute-start(bf16[512,256]{1,0:T(8,128)(2,1)S(1)} %collective-permute-done.7.refs_8_.refs_11_), channel_id=1, source_target_pairs={{0,8},{1,9},{2,10},{3,11},{4,12},{5,13},{6,14},{7,15},{8,16},{9,17... | collective-permute-start | bytes 786440 | tf_op jit(solution)/shard_map/ppermute | solution.py:515
  37.0 15.4 %collective-permute-start.15 = (bf16[512,256]{1,0:T(8,128)(2,1)S(1)}, bf16[512,256]{1,0:T(8,128)(2,1)S(1)}, u32[]{:S(2)}, u32[]{:S(2)}) collective-permute-start(bf16[512,256]{1,0:T(8,128)(2,1)S(1)} %collective-permute-done.7.refs_8_.refs_11_), channel_id=1, source_target_pairs={{0,4},{1,5},{2,6},{3,7},{4,0},{5,1},{6,2},{7,3},{8,12},{9,13},{10,... | collective-permute-start | bytes 786440 | tf_op jit(solution)/shard_map/ppermute | solution.py:515
  38.6 12.4 %collective-permute-start.9 = (bf16[512,256]{1,0:T(8,128)(2,1)S(1)}, bf16[512,256]{1,0:T(8,128)(2,1)S(1)}, u32[]{:S(2)}, u32[]{:S(2)}) collective-permute-start(bf16[512,256]{1,0:T(8,128)(2,1)S(1)} %collective-permute-done.6.refs_5_), channel_id=1, source_target_pairs={{0,8},{1,9},{2,10},{3,11},{4,12},{5,13},{6,14},{7,15},{8,16},{9,17... | collective-permute-start | bytes 786440 | tf_op jit(solution)/shard_map/ppermute | solution.py:515
  48.2 6.0 %copy-start.22 = (f32[4,2,256,128]{3,2,1,0:T(8,128)}, f32[4,2,256,128]{3,2,1,0:T(8,128)S(1)}, u32[]{:S(2)}) copy-start(f32[4,2,256,128]{3,2,1,0:T(8,128)S(1)} %get-tuple-element.36.refs_9_.refs_15_) | copy-start | bytes 3145732
  48.2 6.0 %copy-start.23 = (f32[4,2,256,128]{3,2,1,0:T(8,128)}, f32[4,2,256,128]{3,2,1,0:T(8,128)S(1)}, u32[]{:S(2)}) copy-start(f32[4,2,256,128]{3,2,1,0:T(8,128)S(1)} %get-tuple-element.38.refs_10_.refs_16_) | copy-start | bytes 3145732
  48.2 6.0 %copy-start.24 = (f32[4,2,256,128]{3,2,1,0:T(8,128)}, f32[4,2,256,128]{3,2,1,0:T(8,128)S(1)}, u32[]{:S(2)}) copy-start(f32[4,2,256,128]{3,2,1,0:T(8,128)S(1)} %get-tuple-element.39.refs_11_.refs_17_) | copy-start | bytes 3145732
  48.2 9.1 %collective-permute-start.8 = (bf16[512,256]{1,0:T(8,128)(2,1)S(1)}, bf16[512,256]{1,0:T(8,128)(2,1)S(1)}, u32[]{:S(2)}, u32[]{:S(2)}) collective-permute-start(bf16[512,256]{1,0:T(8,128)(2,1)S(1)} %collective-permute-done.6.refs_5_), channel_id=1, source_target_pairs={{0,4},{1,5},{2,6},{3,7},{4,0},{5,1},{6,2},{7,3},{8,12},{9,13},{10,... | collective-permute-start | bytes 786440 | tf_op jit(solution)/shard_map/ppermute | solution.py:515
  50.9 6.4 %copy-start.8 = (bf16[512,256]{1,0:T(8,128)(2,1)}, bf16[512,256]{1,0:T(8,128)(2,1)S(1)}, u32[]{:S(2)}) copy-start(bf16[512,256]{1,0:T(8,128)(2,1)S(1)} %collective-permute-done.9.refs_4_.refs_7_) | copy-start | bytes 786436
  50.9 9.4 %collective-permute-start.13 = (bf16[512,256]{1,0:T(8,128)(2,1)S(1)}, bf16[512,256]{1,0:T(8,128)(2,1)S(1)}, u32[]{:S(2)}, u32[]{:S(2)}) collective-permute-start(bf16[512,256]{1,0:T(8,128)(2,1)S(1)} %collective-permute-done.9.refs_4_.refs_7_), channel_id=1, source_target_pairs={{0,4},{1,5},{2,6},{3,7},{4,0},{5,1},{6,2},{7,3},{8,12},{9,13},{10,... | collective-permute-start | bytes 786440 | tf_op jit(solution)/shard_map/ppermute | solution.py:515
  52.4 4.9 %copy-start.6 = (bf16[512,256]{1,0:T(8,128)(2,1)}, bf16[512,256]{1,0:T(8,128)(2,1)S(1)}, u32[]{:S(2)}) copy-start(bf16[512,256]{1,0:T(8,128)(2,1)S(1)} %collective-permute-done.15.refs_5_.refs_12_) | copy-start | bytes 786436
  52.4 8.2 %collective-permute-start.16 = (bf16[512,256]{1,0:T(8,128)(2,1)S(1)}, bf16[512,256]{1,0:T(8,128)(2,1)S(1)}, u32[]{:S(2)}, u32[]{:S(2)}) collective-permute-start(bf16[512,256]{1,0:T(8,128)(2,1)S(1)} %collective-permute-done.15.refs_5_.refs_12_), channel_id=1, source_target_pairs={{0,8},{1,9},{2,10},{3,11},{4,12},{5,13},{6,14},{7,15},{8,16},{9,17... | collective-permute-start | bytes 786440 | tf_op jit(solution)/shard_map/ppermute | solution.py:515
  57.4 3.2 %copy-start.10 = (bf16[512,256]{1,0:T(8,128)(2,1)}, bf16[512,256]{1,0:T(8,128)(2,1)S(1)}, u32[]{:S(2)}) copy-start(bf16[512,256]{1,0:T(8,128)(2,1)S(1)} %collective-permute-done.8.refs_3_.refs_6_) | copy-start | bytes 786436
  60.4 4.9 %copy-start.12 = (bf16[512,256]{1,0:T(8,128)(2,1)}, bf16[512,256]{1,0:T(8,128)(2,1)S(1)}, u32[]{:S(2)}) copy-start(bf16[512,256]{1,0:T(8,128)(2,1)S(1)} %collective-permute-done.13.refs_3_.refs_8_) | copy-start | bytes 786436
  60.6 4.6 %copy-start.14 = (bf16[512,256]{1,0:T(8,128)(2,1)}, bf16[512,256]{1,0:T(8,128)(2,1)S(1)}, u32[]{:S(2)}) copy-start(bf16[512,256]{1,0:T(8,128)(2,1)S(1)} %collective-permute-done.16.refs_4_.refs_14_) | copy-start | bytes 786436
  60.6 5.4 %copy-start.25 = (s32[4,8]{1,0:T(4,128)S(1)}, s32[4,8]{1,0:T(4,128)}, u32[]{:S(2)}) copy-start(s32[4,8]{1,0:T(4,128)} %param.29) | copy-start | bytes 388
  65.3 0.8 copy-start.20
  66.0 3.9 %copy-start.7 = (bf16[512,256]{1,0:T(8,128)(2,1)S(1)}, bf16[512,256]{1,0:T(8,128)(2,1)}, u32[]{:S(2)}) copy-start(bf16[512,256]{1,0:T(8,128)(2,1)} %copy-done.6) | copy-start | bytes 786436
  66.0 1.9 %collective-permute-start.17 = (bf16[64,4096]{1,0:T(8,128)(2,1)S(1)}, bf16[64,4096]{1,0:T(8,128)(2,1)S(1)}, u32[]{:S(2)}, u32[]{:S(2)}) collective-permute-start(bf16[64,4096]{1,0:T(8,128)(2,1)S(1)} %get-tuple-element.47), channel_id=1, source_target_pairs={{0,1},{1,0},{2,3},{3,2},{4,5},{5,4},{6,7},{7,6},{8,9},{9,8},{10,11... | collective-permute-start | bytes 1572872 | tf_op jit(solution)/shard_map/ppermute | solution.py:515
  66.2 3.7 %copy-start.9 = (bf16[512,256]{1,0:T(8,128)(2,1)S(1)}, bf16[512,256]{1,0:T(8,128)(2,1)}, u32[]{:S(2)}) copy-start(bf16[512,256]{1,0:T(8,128)(2,1)} %copy-done.8) | copy-start | bytes 786436
  66.2 3.7 %copy-start.11 = (bf16[512,256]{1,0:T(8,128)(2,1)S(1)}, bf16[512,256]{1,0:T(8,128)(2,1)}, u32[]{:S(2)}) copy-start(bf16[512,256]{1,0:T(8,128)(2,1)} %copy-done.10) | copy-start | bytes 786436
  66.2 3.7 %copy-start.13 = (bf16[512,256]{1,0:T(8,128)(2,1)S(1)}, bf16[512,256]{1,0:T(8,128)(2,1)}, u32[]{:S(2)}) copy-start(bf16[512,256]{1,0:T(8,128)(2,1)} %copy-done.12) | copy-start | bytes 786436
  66.2 3.7 %copy-start.15 = (bf16[512,256]{1,0:T(8,128)(2,1)S(1)}, bf16[512,256]{1,0:T(8,128)(2,1)}, u32[]{:S(2)}) copy-start(bf16[512,256]{1,0:T(8,128)(2,1)} %copy-done.14) | copy-start | bytes 786436
  68.0 1.0 %copy-start.21 = (bf16[64,4096]{1,0:T(8,128)(2,1)S(1)}, bf16[64,4096]{1,0:T(8,128)(2,1)}, u32[]{:S(2)}) copy-start(bf16[64,4096]{1,0:T(8,128)(2,1)} %copy-done.20) | copy-start | bytes 1572868
  69.1 0.8 copy-start.3
  69.1 14.6 %collective-permute-start.18 = (bf16[64,4096]{1,0:T(8,128)(2,1)S(1)}, bf16[64,4096]{1,0:T(8,128)(2,1)S(1)}, u32[]{:S(2)}, u32[]{:S(2)}) collective-permute-start(bf16[64,4096]{1,0:T(8,128)(2,1)S(1)} %add_up.3.refs_19_), channel_id=1, source_target_pairs={{0,2},{1,3},{2,0},{3,1},{4,6},{5,7},{6,4},{7,5},{8,10},{9,11},{10,... | collective-permute-start | bytes 1572872 | tf_op jit(solution)/shard_map/ppermute | solution.py:515
  80.9 0.8 copy-start.18
  81.7 3.3 %collective-permute-start.19 = (bf16[64,4096]{1,0:T(8,128)(2,1)}, bf16[64,4096]{1,0:T(8,128)(2,1)S(1)}, u32[]{:S(2)}, u32[]{:S(2)}) collective-permute-start(bf16[64,4096]{1,0:T(8,128)(2,1)} %get-tuple-element.49), channel_id=1, source_target_pairs={{0,1},{1,0},{2,3},{3,2},{4,5},{5,4},{6,7},{7,6},{8,9},{9,8},{10,11... | collective-permute-start | bytes 1572872 | tf_op jit(solution)/shard_map/ppermute | solution.py:515
  83.7 1.0 %copy-start.19 = (bf16[64,4096]{1,0:T(8,128)(2,1)S(1)}, bf16[64,4096]{1,0:T(8,128)(2,1)}, u32[]{:S(2)}) copy-start(bf16[64,4096]{1,0:T(8,128)(2,1)} %copy-done.18) | copy-start | bytes 1572868
